TPU v7x, 128 devices: a whole 4x4x4 slice. The times are simulated.
128 devices in a mesh: ctx: 32 (over y, z, core), rows: 4 (over x).
Axes of the slice: x: 4, y: 4, z: 4, core: 2. Of those that a mesh axis runs over, the one named last changes fastest.
Arguments:
- queries: bfloat16 [256, 2, 8, 1024], P(('ctx', 'rows')), may hold values from -160 to 160
- new_keys: bfloat16 [256, 2, 8, 128], P(('ctx', 'rows')), may hold values from -6 to 6
- new_values: bfloat16 [256, 2, 8, 128], P(('ctx', 'rows')), may hold values from -6 to 6
- recent_keys: bfloat16 [256, 8, 256, 128], P(('ctx', 'rows')), may hold values from -6 to 6
- recent_values: bfloat16 [256, 8, 256, 128], P(('ctx', 'rows')), may hold values from -6 to 6
- page_keys: bfloat16 [8192, 8, 64, 128], P(('ctx', 'rows')), may hold values from -6 to 6
- page_values: bfloat16 [8192, 8, 64, 128], P(('ctx', 'rows')), may hold values from -6 to 6
- page_fill: int32 [8192], P(('ctx', 'rows')), may hold values from 1 to 64
- top_owner: int32 [256, 8, 8], P(('ctx', 'rows')), may hold values from 0 to 127, all different within a row; in each aligned block of 16 rows (0 to 15, 16 to 31, ..., all dimensions but the last counted through in order) at most 2 rows name the same one
- top_slot: int32 [256, 8, 8], P(('ctx', 'rows')), may hold values from 0 to 63
Outputs:
- attended: bfloat16 [256, 2, 8, 1024], P(('ctx', 'rows'))
Inputs may be any that keep to these rules, and one draw needn't show every extreme that they name: `top_owner`: each row names 8 different devices for one key-value head; in the rows of one device (aligned blocks of 16 rows of the first two dimensions) no device is named more than 2 times.
All inputs are finite; a program needn't handle non-finite values.
Results may differ from a plain program's by a relative error of at most 0.009.
Values may be sent and summed in bfloat16 or wider, within the bound.
No kernel may reach another device: no remote copies, remote signals or barrier semaphores. Data moves between devices by JAX's collectives and lax.ppermute only.
A program may use at most 128 MiB of HBM per device.

v0:
```python
import jax
import jax.numpy as jnp
from jax import lax
from jax.sharding import PartitionSpec as P

SCORE_FLOOR = -1e30


def page_partials(query_tiles, got_keys, got_values, filled, is_valid):
    score_scale = query_tiles.shape[-1] ** (-0.5)
    scores = (
        jnp.einsum("mqd,mjd->mqj", query_tiles, got_keys, preferred_element_type=jnp.float32)
        * score_scale
    )
    token_index = lax.broadcasted_iota(jnp.int32, scores.shape, 2)
    scores = jnp.where(token_index < filled[:, None, None], scores, SCORE_FLOOR)
    peak_score = jnp.max(scores, axis=2)
    weights = jnp.exp(scores - peak_score[:, :, None])
    weight_sum = jnp.sum(weights, axis=2)
    summed = jnp.einsum("mqj,mjd->mqd", weights, got_values.astype(jnp.float32))
    peak_score = jnp.where(is_valid[:, None], peak_score, SCORE_FLOOR)
    return (summed, peak_score, weight_sum)


def on_device(
    queries,
    new_keys,
    new_values,
    recent_keys,
    recent_values,
    page_keys,
    page_values,
    page_fill,
    top_owner,
    top_slot,
):
    seq_count, step_count, head_count, _ = queries.shape
    head_size = new_keys.shape[3]
    group_size = queries.shape[3] // head_size
    pick_count = top_owner.shape[2]
    tile_rows = step_count * group_size
    devices = lax.axis_size(("ctx", "rows"))
    item_count = seq_count * head_count * pick_count
    capacity = max(2, 2 * item_count // devices)
    score_scale = head_size ** (-0.5)
    query_tiles = queries.reshape(seq_count, step_count, head_count, group_size, head_size)
    query_tiles = jnp.transpose(query_tiles, (0, 2, 1, 3, 4)).reshape(
        seq_count, head_count, tile_rows, head_size
    )
    owners = top_owner.reshape(item_count)
    one_hot = (owners[:, None] == jnp.arange(devices, dtype=jnp.int32)[None, :]).astype(jnp.int32)
    before = jnp.cumsum(one_hot, axis=0) - one_hot
    placed = jnp.sum(before * one_hot, axis=1)
    target = owners * capacity + placed
    head_ids = jnp.arange(head_count, dtype=jnp.int32)[None, :, None]
    request_code = (top_slot * head_count + head_ids + 1).reshape(item_count)
    item_tiles = jnp.broadcast_to(
        query_tiles[:, :, None], (seq_count, head_count, pick_count, tile_rows, head_size)
    )
    item_tiles = item_tiles.reshape(item_count, tile_rows, head_size)
    near_scores = (
        jnp.einsum("sgqd,sgjd->sgqj", query_tiles, recent_keys, preferred_element_type=jnp.float32)
        * score_scale
    )
    fresh_keys = jnp.transpose(new_keys, (0, 2, 1, 3))
    fresh_values = jnp.transpose(new_values, (0, 2, 1, 3))
    fresh_scores = (
        jnp.einsum("sgqd,sgud->sgqu", query_tiles, fresh_keys, preferred_element_type=jnp.float32)
        * score_scale
    )
    query_step = lax.broadcasted_iota(jnp.int32, fresh_scores.shape, 2) // group_size
    fresh_index = lax.broadcasted_iota(jnp.int32, fresh_scores.shape, 3)
    fresh_scores = jnp.where(fresh_index <= query_step, fresh_scores, SCORE_FLOOR)
    local_peak = jnp.maximum(jnp.max(near_scores, axis=3), jnp.max(fresh_scores, axis=3))
    near_weights = jnp.exp(near_scores - local_peak[..., None])
    fresh_weights = jnp.exp(fresh_scores - local_peak[..., None])
    local_sum = jnp.sum(near_weights, axis=3) + jnp.sum(fresh_weights, axis=3)
    local_summed = jnp.einsum("sgqj,sgjd->sgqd", near_weights, recent_values.astype(jnp.float32))
    local_summed = local_summed + jnp.einsum(
        "sgqu,sgud->sgqd", fresh_weights, fresh_values.astype(jnp.float32)
    )
    request = (
        jnp.zeros((devices * capacity,), jnp.int32)
        .at[target]
        .set(request_code)
        .reshape(devices, capacity)
    )
    wanted = jnp.maximum(
        lax.all_to_all(request, ("ctx", "rows"), split_axis=0, concat_axis=0, tiled=True) - 1, 0
    )
    page_slot = wanted // head_count
    kv_head = wanted % head_count
    got_keys = lax.all_to_all(
        page_keys[page_slot, kv_head], ("ctx", "rows"), split_axis=0, concat_axis=0, tiled=True
    )
    got_values = lax.all_to_all(
        page_values[page_slot, kv_head], ("ctx", "rows"), split_axis=0, concat_axis=0, tiled=True
    )
    filled = lax.all_to_all(
        page_fill[page_slot], ("ctx", "rows"), split_axis=0, concat_axis=0, tiled=True
    )
    got_keys = got_keys.reshape((devices * capacity,) + got_keys.shape[2:])[target]
    got_values = got_values.reshape((devices * capacity,) + got_values.shape[2:])[target]
    filled = filled.reshape(devices * capacity)[target]
    item_summed, item_peak, item_sum = page_partials(
        item_tiles, got_keys, got_values, filled, jnp.ones((item_count,), jnp.bool_)
    )
    item_summed = item_summed.reshape(seq_count, head_count, pick_count, tile_rows, head_size)
    item_peak = item_peak.reshape(seq_count, head_count, pick_count, tile_rows)
    item_sum = item_sum.reshape(seq_count, head_count, pick_count, tile_rows)
    overall_peak = jnp.maximum(local_peak, jnp.max(item_peak, axis=2))
    local_factor = jnp.exp(local_peak - overall_peak)
    item_factor = jnp.exp(item_peak - overall_peak[:, :, None])
    total_sum = local_sum * local_factor + jnp.sum(item_sum * item_factor, axis=2)
    total_summed = local_summed * local_factor[..., None] + jnp.sum(
        item_summed * item_factor[..., None], axis=2
    )
    mixed = total_summed / total_sum[..., None]
    mixed = mixed.reshape(seq_count, head_count, step_count, group_size, head_size)
    mixed = jnp.transpose(mixed, (0, 2, 1, 3, 4)).reshape(
        seq_count, step_count, head_count, group_size * head_size
    )
    return mixed.astype(jnp.bfloat16)


def solution(mesh):
    return jax.shard_map(
        on_device,
        mesh=mesh,
        in_specs=(
            P(("ctx", "rows"), None, None, None),
            P(("ctx", "rows"), None, None, None),
            P(("ctx", "rows"), None, None, None),
            P(("ctx", "rows"), None, None, None),
            P(("ctx", "rows"), None, None, None),
            P(("ctx", "rows"), None, None, None),
            P(("ctx", "rows"), None, None, None),
            P(("ctx", "rows")),
            P(("ctx", "rows"), None, None),
            P(("ctx", "rows"), None, None),
        ),
        out_specs=P(("ctx", "rows"), None, None, None),
        check_vma=False,
    )
```

profile of v0, /device:TPU:1, one launch (start us, length us, event | category | flops | bytes accessed | tf_op | source)
XLA Modules:
  0.0 170.3 jit_solution(1680489770393455768)
XLA Ops:
  0.0 0.0 copy-start
  0.0 0.9 eq.17
  0.9 0.7 broadcast_multiply_fusion
  1.6 0.1 fusion.14
  1.7 0.2 reduce_window_sum.11
  1.9 0.2 select_reduce_fusion
  2.0 0.1 mul.78
  2.1 0.7 add_add_fusion
  2.8 0.1 reshape.262
  2.9 1.0 scatter_custom_fusion
  3.9 0.1 all_to_all.18
  4.1 21.2 %all_to_all.28 = s32[128,1,2]{2,1,0:T(1,128)S(1)} all-to-all(s32[128,1,2]{2,1,0:T(1,128)S(1)} %bitcast.85), channel_id=1, replica_groups=mesh['ctx'=32,'rows'=4] {'ctx','rows'}, dimensions={0} | all-to-all | bytes 2048 | tf_op jit(solution)/shard_map/all_to_all | solution.py:89
  25.3 0.1 copy.33
  25.4 0.1 copy.34
  25.5 0.1 reshape.216
  25.6 0.0 copy-done.1
  25.6 1.9 %gather_fusion = s32[256]{0:T(256)S(1)} fusion(s32[64]{0:T(128)S(1)} %copy-done.1, s32[1024]{0:T(1024)S(1)} %pad_clamp_fusion.1), kind=kCustom, calls=%fused_computation | custom fusion | bytes 3072 | tf_op jit(solution)/shard_map/gather | solution.py:100
  27.5 0.8 all_to_all.20
  28.3 4.1 %all-to-all-start.1 = ((s32[128,1,2]{2,1,0:T(1,128)}), s32[128,1,2]{2,1,0:T(1,128)S(1)}, u32[]{:S(2)}, u32[]{:S(2)}) async-start(s32[128,1,2]{2,1,0:T(1,128)} %bitcast.11), calls=%async_computation.1 | async-start | bytes 131072 | tf_op jit(solution)/shard_map/all_to_all | solution.py:99
  32.3 0.1 copy.36
  32.5 0.1 reshape.230
  32.6 6.7 %gather_fusion.2 = bf16[256,64,128]{2,1,0:T(8,128)(2,1)} fusion(bf16[64,8,64,128]{3,2,1,0:T(8,128)(2,1)} %param.15, s32[256]{0:T(256)S(1)} %reshape.230), kind=kCustom, calls=%fused_computation.2 | custom fusion | bytes 8390656 | tf_op jit(solution)/shard_map/gather | solution.py:94
  39.3 2.9 %all-to-all-done.1 = s32[128,1,2]{2,1,0:T(1,128)S(1)} async-done(((s32[128,1,2]{2,1,0:T(1,128)}), s32[128,1,2]{2,1,0:T(1,128)S(1)}, u32[]{:S(2)}, u32[]{:S(2)}) %all-to-all-start.1) | async-done | bytes 1056 | tf_op jit(solution)/shard_map/all_to_all | solution.py:99
  42.2 7.4 %all-to-all-start.2 = ((bf16[128,2,64,128]{3,2,1,0:T(8,128)(2,1)}), bf16[128,2,64,128]{3,2,1,0:T(8,128)(2,1)}, u32[]{:S(2)}, u32[]{:S(2)}) async-start(bf16[128,2,64,128]{3,2,1,0:T(8,128)(2,1)} %bitcast.82), calls=%async_computation.2 | async-start | bytes 8388608 | tf_op jit(solution)/shard_map/all_to_all | solution.py:93
  49.5 6.7 %gather_fusion.4 = bf16[256,64,128]{2,1,0:T(8,128)(2,1)} fusion(bf16[64,8,64,128]{3,2,1,0:T(8,128)(2,1)} %param.16, s32[256]{0:T(256)S(1)} %reshape.230), kind=kCustom, calls=%fused_computation.4 | custom fusion | bytes 8390656 | tf_op jit(solution)/shard_map/gather | solution.py:97
  56.3 46.4 %all-to-all-done.2 = bf16[128,2,64,128]{3,2,1,0:T(8,128)(2,1)} async-done(((bf16[128,2,64,128]{3,2,1,0:T(8,128)(2,1)}), bf16[128,2,64,128]{3,2,1,0:T(8,128)(2,1)}, u32[]{:S(2)}, u32[]{:S(2)}) %all-to-all-start.2) | async-done | bytes 4194336 | tf_op jit(solution)/shard_map/all_to_all | solution.py:93
  102.6 5.0 %all-to-all-start.3 = ((bf16[128,2,64,128]{3,2,1,0:T(8,128)(2,1)}), bf16[128,2,64,128]{3,2,1,0:T(8,128)(2,1)}, u32[]{:S(2)}, u32[]{:S(2)}) async-start(bf16[128,2,64,128]{3,2,1,0:T(8,128)(2,1)} %bitcast.81), calls=%async_computation.3 | async-start | bytes 8388608 | tf_op jit(solution)/shard_map/all_to_all | solution.py:96
  107.7 0.2 fusion.31
  107.9 0.0 copy-start.4
  107.9 0.4 fusion.30
  108.3 0.6 broadcast.289
  108.9 0.8 reduce.3
  109.7 0.1 reshape.208
  109.8 1.3 gather_fusion.1
  111.1 4.4 %gather_fusion.3 = bf16[128,64,128]{2,1,0:T(8,128)(2,1)} fusion(bf16[256,64,128]{2,1,0:T(8,128)(2,1)} %bitcast.13, s32[1024]{0:T(1024)S(1)} %pad_clamp_fusion), kind=kCustom, calls=%fused_computation.3 | custom fusion | bytes 4194816 | tf_op jit(solution)/shard_map/gather | solution.py:102
  115.4 0.1 broadcast_in_dim.17
  115.5 2.9 %fusion.29 = (f32[128,16]{1,0:T(8,128)S(1)}, f32[128,16,64]{2,1,0:T(8,128)S(1)}) fusion(bf16[128,64,128]{2,1,0:T(8,128)(2,1)} %gather_fusion.3, bf16[128,16,128]{2,1,0:T(8,128)(2,1)S(1)} %bitcast.83, s32[128]{0:T(128)S(1)} %gather_fusion.1), kind=kOutput, calls=%fused_computation.70 | convolution fusion | flops 34076672 | bytes 3154432 | tf_op jit(solution)/shard_map/mqd,mjd->mqj/dot_general | solution.py:12
  118.5 0.6 fusion.15
  119.1 0.8 fusion.11
  119.9 0.7 fusion.8
  120.5 0.0 copy-start.2
  120.6 40.3 %all-to-all-done.3 = bf16[128,2,64,128]{3,2,1,0:T(8,128)(2,1)} async-done(((bf16[128,2,64,128]{3,2,1,0:T(8,128)(2,1)}), bf16[128,2,64,128]{3,2,1,0:T(8,128)(2,1)}, u32[]{:S(2)}, u32[]{:S(2)}) %all-to-all-start.3) | async-done | bytes 4194336 | tf_op jit(solution)/shard_map/all_to_all | solution.py:96
  160.8 4.5 %gather_fusion.5 = bf16[128,64,128]{2,1,0:T(8,128)(2,1)} fusion(bf16[256,64,128]{2,1,0:T(8,128)(2,1)} %bitcast.18, s32[1024]{0:T(1024)} %copy-done.5), kind=kCustom, calls=%fused_computation.5 | custom fusion | bytes 4194816 | tf_op jit(solution)/shard_map/gather | solution.py:103
  165.3 0.9 fusion.16
  166.3 2.4 %multiply_reduce_fusion = f32[2,8,16,128]{3,2,1,0:T(8,128)S(1)} fusion(f32[2,8,8,16]{3,2,1,0:T(8,128)S(1)} %get-tuple-element.8, bf16[128,64,128]{2,1,0:T(8,128)(2,1)} %gather_fusion.5, f32[128,16,64]{2,1,0:T(8,128)S(1)} %get-tuple-element.14, f32[128,16]{1,0:T(8,128)S(1)} %get-tuple-element.13), kind=kOutput, calls=%fused_computation.19 | convolution fusion | flops 34177024 | bytes 2768896 | tf_op jit(solution)/shard_map/mqj,mjd->mqd/dot_general | solution.py:20
  168.6 0.7 multiply_add_fusion
  169.4 0.3 fusion.6
  169.7 0.7 copy.52
  (20 shorter events, 0.2 us)
Async XLA Ops:
  0.0 107.9 %copy-start = (bf16[2,8,256,128]{3,2,1,0:T(8,128)(2,1)S(1)}, bf16[2,8,256,128]{3,2,1,0:T(8,128)(2,1)}, u32[]{:S(2)}) copy-start(bf16[2,8,256,128]{3,2,1,0:T(8,128)(2,1)} %param.13) | copy-start | bytes 3145732
  0.0 25.6 %copy-start.1 = (s32[64]{0:T(128)S(1)}, s32[64]{0:T(128)}, u32[]{:S(2)}) copy-start(s32[64]{0:T(128)} %param.17) | copy-start | bytes 772
  28.3 13.9 %all-to-all-start.1 = ((s32[128,1,2]{2,1,0:T(1,128)}), s32[128,1,2]{2,1,0:T(1,128)S(1)}, u32[]{:S(2)}, u32[]{:S(2)}) async-start(s32[128,1,2]{2,1,0:T(1,128)} %bitcast.11), calls=%async_computation.1 | async-start | bytes 131072 | tf_op jit(solution)/shard_map/all_to_all | solution.py:99
  42.2 60.5 %all-to-all-start.2 = ((bf16[128,2,64,128]{3,2,1,0:T(8,128)(2,1)}), bf16[128,2,64,128]{3,2,1,0:T(8,128)(2,1)}, u32[]{:S(2)}, u32[]{:S(2)}) async-start(bf16[128,2,64,128]{3,2,1,0:T(8,128)(2,1)} %bitcast.82), calls=%async_computation.2 | async-start | bytes 8388608 | tf_op jit(solution)/shard_map/all_to_all | solution.py:93
  102.6 5.0 %copy-start.3 = (bf16[2,2,8,1024]{3,2,1,0:T(8,128)(2,1)S(1)}, bf16[2,2,8,1024]{3,2,1,0:T(8,128)(2,1)}, u32[]{:S(2)}) copy-start(bf16[2,2,8,1024]{3,2,1,0:T(8,128)(2,1)} %param.10) | copy-start | bytes 196612
  102.6 5.1 %copy-start.6 = (bf16[2,2,8,128]{3,2,1,0:T(8,128)(2,1)S(1)}, bf16[2,2,8,128]{3,2,1,0:T(8,128)(2,1)}, u32[]{:S(2)}) copy-start(bf16[2,2,8,128]{3,2,1,0:T(8,128)(2,1)} %param.11) | copy-start | bytes 24580
  102.6 58.2 %all-to-all-start.3 = ((bf16[128,2,64,128]{3,2,1,0:T(8,128)(2,1)}), bf16[128,2,64,128]{3,2,1,0:T(8,128)(2,1)}, u32[]{:S(2)}, u32[]{:S(2)}) async-start(bf16[128,2,64,128]{3,2,1,0:T(8,128)(2,1)} %bitcast.81), calls=%async_computation.3 | async-start | bytes 8388608 | tf_op jit(solution)/shard_map/all_to_all | solution.py:96
  107.7 10.7 %copy-start.5 = (s32[1024]{0:T(1024)}, s32[1024]{0:T(1024)S(1)}, u32[]{:S(2)}) copy-start(s32[1024]{0:T(1024)S(1)} %pad_clamp_fusion) | copy-start | bytes 12292
  107.9 10.6 %copy-start.4 = (f32[2,8,16,2]{2,3,1,0:T(2,128)}, f32[2,8,16,2]{2,3,1,0:T(2,128)S(1)}, u32[]{:S(2)}) copy-start(f32[2,8,16,2]{2,3,1,0:T(2,128)S(1)} %get-tuple-element.18) | copy-start | bytes 6148
  120.5 48.8 %copy-start.2 = (bf16[2,8,256,128]{3,2,1,0:T(8,128)(2,1)S(1)}, bf16[2,8,256,128]{3,2,1,0:T(8,128)(2,1)}, u32[]{:S(2)}) copy-start(bf16[2,8,256,128]{3,2,1,0:T(8,128)(2,1)} %param.14) | copy-start | bytes 3145732
where the time goes:
time: 171 us; the launch traced here: 170 us
  waiting for transfers between devices  89.5 us (52%)
  local copies, waits for them, and re-layouts  30.4 us (18%)
  blocking collectives  21.2 us (12%)
  starting transfers between devices  16.4 us (10%)
  matrix products  7.08 us (4%)
  other arithmetic  5.56 us (3%)
    all_to_all x1, waiting for transfers between devices, on_device(): lax.all_to_all(page_keys[page_slot, kv_head], ('ctx', 'rows'), split_axis...  46.4 us
    all_to_all x1, waiting for transfers between devices, on_device(): lax.all_to_all(page_values[page_slot, kv_head], ('ctx', 'rows'), split_ax...  40.3 us
    all_to_all x1, blocking collectives, on_device(): lax.all_to_all(request, ('ctx', 'rows'), split_axis=0, concat_axis=0, til...  21.2 us
    all_to_all x1, starting transfers between devices, on_device(): lax.all_to_all(page_keys[page_slot, kv_head], ('ctx', 'rows'), split_axis...  7.36 us
    gather x1, local copies, waits for them, and re-layouts, on_device(): page_values[page_slot, kv_head]  6.74 us
    gather x1, local copies, waits for them, and re-layouts, on_device(): page_keys[page_slot, kv_head]  6.7 us
    all_to_all x1, starting transfers between devices, on_device(): lax.all_to_all(page_values[page_slot, kv_head], ('ctx', 'rows'), split_ax...  4.96 us
    gather x1, local copies, waits for them, and re-layouts, on_device(): got_values.reshape((devices * capacity,) + got_values.shape[2:])[target]  4.45 us
  transfers between devices with their start and end apart: 3, of which 3 were waited for; matrix products, arithmetic and copies ran while one was open for 16% of the time, Pallas kernels for 0%

commit v1 on v0

v1 whole, which is shorter than its diff:
```python
import functools

import jax
import jax.numpy as jnp
from jax import lax
from jax.experimental import pallas as pl
from jax.experimental.pallas import tpu as pltpu
from jax.sharding import PartitionSpec as P

AXES = ("ctx", "rows")
FLOOR = -1e30
LANES = 128
SLOTS = 2
TILE = 16
SPAN = SLOTS * TILE + SLOTS
MIB = 1024 * 1024


def lane_iota(rows):
    return lax.broadcasted_iota(jnp.int32, (rows, LANES), 1)


def row_iota(rows):
    return lax.broadcasted_iota(jnp.int32, (rows, LANES), 0)


def load_tiles(queries, tiles):
    seqs, steps, kv, wide = queries.shape
    group = wide // LANES
    for s in range(seqs):
        for t in range(steps):
            for h in range(group):
                block = queries[s, t, :, h * LANES : (h + 1) * LANES]
                start = s * kv * TILE + t * group + h
                tiles[pl.ds(start, kv, stride=TILE), :] = block.astype(jnp.float32)


def pack_kernel(picks, owner, slot, queries, out, place, tiles, wide, count):
    devices = wide.shape[0] // SPAN
    kv = queries.shape[2]
    load_tiles(queries, tiles)
    wide[...] = jnp.zeros_like(wide)

    def clear(i, carry):
        count[i] = 0
        return carry

    lax.fori_loop(0, devices, clear, 0, unroll=16)
    lane = lane_iota(1)

    def fill_tile(tile, carry):
        block = tiles[pl.ds(pl.multiple_of(tile * TILE, TILE), TILE), :]
        head = lax.rem(tile, kv)
        for k in range(picks):
            item = tile * picks + k
            to = owner[item]
            used = count[to]
            count[to] = used + 1
            place[item] = to * SLOTS + used
            base = to * SPAN
            wide[pl.ds(base + used * TILE, TILE), :] = block
            code = jnp.where(lane < LANES // 2, slot[item], head).astype(jnp.float32)
            wide[pl.ds(base + SLOTS * TILE + used, 1), :] = code
        return carry

    lax.fori_loop(0, tiles.shape[0] // TILE, fill_tile, 0, unroll=2)
    out[...] = wide[...].astype(out.dtype)


def local_kernel(queries, new_keys, new_values, keys, values, mixed, level, tiles, fresh):
    seqs, steps, kv, wide = queries.shape
    group = wide // LANES
    recent = keys.shape[2]
    scale = LANES ** (-0.5)
    load_tiles(queries, tiles)
    news = seqs * steps * kv
    for s in range(seqs):
        for u in range(steps):
            at = (s * steps + u) * kv
            fresh[at : at + kv, :] = new_keys[s, u].astype(jnp.float32)
            fresh[news + at : news + at + kv, :] = new_values[s, u].astype(jnp.float32)
    fresh_keys = fresh[:news, :].astype(jnp.bfloat16)
    fresh_values = jnp.concatenate(
        [fresh[news:, :].astype(jnp.bfloat16), jnp.ones((news, LANES), jnp.bfloat16)], axis=1
    )
    ones = jnp.ones((recent, LANES), jnp.bfloat16)
    col = lax.broadcasted_iota(jnp.int32, (TILE, news), 1)
    step = lax.broadcasted_iota(jnp.int32, (TILE, news), 0) // group
    nt = (((1,), (1,)), ((), ()))
    for s in range(seqs):
        for g in range(kv):
            at = (s * kv + g) * TILE
            query = tiles[at : at + TILE, :].astype(jnp.bfloat16)
            near = lax.dot_general(query, keys[s, g], nt, preferred_element_type=jnp.float32) * scale
            late = lax.dot_general(query, fresh_keys, nt, preferred_element_type=jnp.float32) * scale
            first = s * steps * kv + g
            seen = (col >= first) & (col <= first + step * kv) & (lax.rem(col, kv) == g)
            late = jnp.where(seen, late, FLOOR)
            peak = jnp.maximum(
                jnp.max(near, axis=1, keepdims=True), jnp.max(late, axis=1, keepdims=True)
            )
            near_weights = jnp.exp(near - peak).astype(jnp.bfloat16)
            late_weights = jnp.exp(late - peak).astype(jnp.bfloat16)
            both = jnp.concatenate([values[s, g], ones], axis=1)
            total = lax.dot(near_weights, both, preferred_element_type=jnp.float32)
            total = total + lax.dot(late_weights, fresh_values, preferred_element_type=jnp.float32)
            weight = total[:, LANES:]
            mixed[at : at + TILE, :] = total[:, :LANES] / weight
            level[at : at + TILE, :] = peak + jnp.log(weight)


def read_codes(wide, codes):
    devices = wide.shape[0] // SPAN
    half = LANES // 2
    lane = lane_iota(1)
    rows = []
    heads = []
    for c in range(SLOTS):
        low = jnp.zeros((8, LANES), jnp.float32)
        high = jnp.zeros((8, LANES), jnp.float32)
        for j in range(devices // 8):
            start = j * 8 * SPAN + SLOTS * TILE + c
            block = wide[pl.ds(start, 8, stride=SPAN), :]
            mine = lax.rem(lane_iota(8), half) == lax.rem(row_iota(8) + j * 8, half)
            block = jnp.where(mine, block, 0.0)
            if j * 8 < half:
                low = low + block
            else:
                high = high + block
        low = jnp.sum(low, axis=0, keepdims=True)
        high = jnp.sum(high, axis=0, keepdims=True)
        rows.append(jnp.where(lane < half, low, pltpu.roll(high, half, 1)))
        heads.append(jnp.where(lane < half, pltpu.roll(low, half, 1), high))
    for i, row in enumerate(rows + heads):
        codes[i : i + 1, :] = row.astype(jnp.int32)


def answer_kernel(kv, fill, got, keys, values, out, wide, answer, codes_v, codes, sem):
    devices = wide.shape[0] // SPAN
    page = keys.shape[1]
    scale = LANES ** (-0.5)
    wide[...] = got[...].astype(jnp.float32)
    codes_v[...] = jnp.zeros_like(codes_v)
    read_codes(wide, codes_v)
    copy = pltpu.make_async_copy(codes_v, codes, sem)
    copy.start()
    copy.wait()
    nt = (((1,), (1,)), ((), ()))
    lane = lane_iota(TILE)
    row = row_iota(TILE)
    group = 4
    ones = jnp.ones((group * page, LANES), jnp.bfloat16)
    blank = jnp.zeros((TILE, LANES), jnp.float32)
    piece = lane // TILE
    mine = lax.rem(lane, TILE) == row

    def attend(step, carry):
        spots, fills, queries, page_keys, page_values = [], [], [], [], []
        for a in range(group):
            message = step * (group // SLOTS) + a // SLOTS
            c = a % SLOTS
            number = codes[c, message]
            where = number * kv + codes[SLOTS + c, message]
            spots.append((message * SPAN + c * TILE, message * SPAN + SLOTS * TILE + c))
            fills.append(fill[number])
            queries.append(wide[pl.ds(spots[a][0], TILE), :].astype(jnp.bfloat16))
            page_keys.append(keys[where])
            page_values.append(values[where])
        scores = lax.dot_general(
            jnp.concatenate(queries, axis=0),
            jnp.concatenate(page_keys, axis=0),
            nt,
            preferred_element_type=jnp.float32,
        )
        weights, peaks = [], []
        for a in range(group):
            column = a * page // LANES
            first = a * page % LANES
            part = scores[a * TILE : (a + 1) * TILE, column * LANES : (column + 1) * LANES] * scale
            live = (lane >= first) & (lane < first + fills[a])
            part = jnp.where(live, part, FLOOR)
            peak = jnp.max(part, axis=1, keepdims=True)
            part = jnp.exp(part - peak)
            peaks.append(peak)
            line = [blank] * (group * page // LANES)
            line[column] = part
            weights.append(jnp.concatenate(line, axis=1))
        weights = jnp.concatenate(weights, axis=0).astype(jnp.bfloat16)
        both = jnp.concatenate([jnp.concatenate(page_values, axis=0), ones], axis=1)
        total = lax.dot(weights, both, preferred_element_type=jnp.float32)
        for a in range(group):
            part = total[a * TILE : (a + 1) * TILE, :]
            weight = part[:, LANES:]
            answer[pl.ds(spots[a][0], TILE), :] = part[:, :LANES] / weight
            level = peaks[a] + jnp.log(weight)
            high = level.astype(jnp.bfloat16).astype(jnp.float32)
            rest = level - high
            middle = rest.astype(jnp.bfloat16).astype(jnp.float32)
            low = rest - middle
            side = jnp.where(piece == 0, high, jnp.where(piece == 1, middle, low))
            side = jnp.where(mine & (piece < 3), side, 0.0)
            answer[pl.ds(spots[a][1], 1), :] = jnp.sum(side, axis=0, keepdims=True)
        return carry

    lax.fori_loop(0, devices * SLOTS // group, attend, 0, unroll=2)
    out[...] = answer[...].astype(out.dtype)


def merge_kernel(picks, place, got, mixed, level, out, wide, merged):
    seqs, steps, kv, width = out.shape
    group = width // LANES
    wide[...] = got[...].astype(jnp.float32)
    lane = lane_iota(TILE)
    mine = (lax.rem(lane, TILE) == row_iota(TILE)) & (lane < 3 * TILE)
    ones = jnp.ones((LANES, LANES), jnp.bfloat16)

    def merge(tile, carry):
        at = pl.multiple_of(tile * TILE, TILE)
        sides, parts = [], []
        for k in range(picks):
            spot = place[tile * picks + k]
            message = spot // SLOTS
            c = lax.rem(spot, SLOTS)
            parts.append(wide[pl.ds(message * SPAN + c * TILE, TILE), :])
            side = wide[pl.ds(message * SPAN + SLOTS * TILE + c, 1), :]
            sides.append(jnp.where(mine, side, 0.0))
        sides = jnp.concatenate(sides, axis=0).astype(jnp.bfloat16)
        levels = lax.dot(sides, ones, preferred_element_type=jnp.float32)
        levels = [levels[k * TILE : (k + 1) * TILE, :] for k in range(picks)]
        levels.append(level[pl.ds(at, TILE), :])
        parts.append(mixed[pl.ds(at, TILE), :])
        top = functools.reduce(jnp.maximum, levels)
        shares = [jnp.exp(x - top) for x in levels]
        total = functools.reduce(jnp.add, [w * x for w, x in zip(shares, parts)])
        merged[pl.ds(at, TILE), :] = total / functools.reduce(jnp.add, shares)
        return carry

    lax.fori_loop(0, merged.shape[0] // TILE, merge, 0, unroll=2)
    for s in range(seqs):
        for t in range(steps):
            for h in range(group):
                start = s * kv * TILE + t * group + h
                block = merged[pl.ds(start, kv, stride=TILE), :]
                out[s, t, :, h * LANES : (h + 1) * LANES] = block.astype(out.dtype)


VMEM = pl.BlockSpec(memory_space=pltpu.VMEM)
SMEM = pl.BlockSpec(memory_space=pltpu.SMEM)


def params(limit):
    return pltpu.CompilerParams(vmem_limit_bytes=limit * MIB)


def exchange(messages, devices):
    boxed = messages.reshape(devices, SPAN // 2, 2, LANES)
    boxed = lax.all_to_all(boxed, AXES, split_axis=0, concat_axis=0, tiled=True)
    return boxed.reshape(devices * SPAN, LANES)


def on_device(
    queries,
    new_keys,
    new_values,
    recent_keys,
    recent_values,
    page_keys,
    page_values,
    page_fill,
    top_owner,
    top_slot,
):
    seqs, steps, kv, width = queries.shape
    picks = top_owner.shape[2]
    items = seqs * kv * picks
    devices = lax.axis_size(AXES)
    rows = devices * SPAN
    tile_rows = seqs * kv * TILE
    wide = pltpu.VMEM((rows, LANES), jnp.float32)
    tiles = pltpu.VMEM((tile_rows, LANES), jnp.float32)
    messages = jax.ShapeDtypeStruct((rows, LANES), jnp.bfloat16)

    asked, place = pl.pallas_call(
        functools.partial(pack_kernel, picks),
        out_shape=(messages, jax.ShapeDtypeStruct((items,), jnp.int32)),
        in_specs=[SMEM, SMEM, VMEM],
        out_specs=(VMEM, SMEM),
        scratch_shapes=[tiles, wide, pltpu.SMEM((devices,), jnp.int32)],
        compiler_params=params(16),
        name="pack",
    )(top_owner.reshape(items), top_slot.reshape(items), queries)
    asked = exchange(asked, devices)

    near = jax.ShapeDtypeStruct((tile_rows, LANES), jnp.float32)
    mixed, level = pl.pallas_call(
        local_kernel,
        out_shape=(near, near),
        in_specs=[VMEM] * 5,
        out_specs=(VMEM, VMEM),
        scratch_shapes=[tiles, pltpu.VMEM((2 * seqs * steps * kv, LANES), jnp.float32)],
        compiler_params=params(16),
        cost_estimate=pl.CostEstimate(flops=70_000_000, bytes_accessed=3_000_000, transcendentals=70_000),
        name="near",
    )(queries, new_keys, new_values, recent_keys, recent_values)

    pages = page_keys.shape[0] * kv
    pool = (pages, page_keys.shape[2], LANES)
    answers = pl.pallas_call(
        functools.partial(answer_kernel, kv),
        out_shape=messages,
        in_specs=[SMEM, VMEM, VMEM, VMEM],
        out_specs=VMEM,
        scratch_shapes=[
            wide,
            wide,
            pltpu.VMEM((8, LANES), jnp.int32),
            pltpu.SMEM((8, LANES), jnp.int32),
            pltpu.SemaphoreType.DMA,
        ],
        compiler_params=params(16),
        name="answer",
    )(
        page_fill,
        asked,
        pltpu.with_memory_space_constraint(page_keys.reshape(pool), pltpu.VMEM),
        pltpu.with_memory_space_constraint(page_values.reshape(pool), pltpu.VMEM),
    )
    answers = exchange(answers, devices)

    return pl.pallas_call(
        functools.partial(merge_kernel, picks),
        out_shape=jax.ShapeDtypeStruct(queries.shape, jnp.bfloat16),
        in_specs=[SMEM, VMEM, VMEM, VMEM],
        out_specs=VMEM,
        scratch_shapes=[wide, tiles],
        compiler_params=params(16),
        name="merge",
    )(place, answers, mixed, level)


def solution(mesh):
    split = P(AXES)
    return jax.shard_map(
        on_device,
        mesh=mesh,
        in_specs=(split,) * 10,
        out_specs=split,
        check_vma=False,
    )
```

time: 171 us -> 88.8 us (0.52)
  waiting for transfers between devices: 89.5 us -> 17.1 us
  Pallas kernels: 0 us -> 25.3 us
  local copies, waits for them, and re-layouts: 30.4 us -> 10.4 us
  starting transfers between devices: 16.4 us -> 3.81 us
  blocking collectives: 21.2 us -> 31.7 us
  matrix products: 7.08 us -> 0 us
  other arithmetic: 5.56 us -> 0 us
    all_to_all x3 -> x1, waiting for transfers between devices: 89.5 us -> 17.1 us  [exchange(): boxed = lax.all_to_all(boxed, AXES, split_axis=0, concat_axis=0, tiled=True)]
    gather x6 -> x0, local copies, waits for them, and re-layouts: 25.4 us -> none  [the longest x1 6.74 us: on_device(): page_values[page_slot, kv_head]]
    pallas_call x0 -> x4, Pallas kernels: none -> 25.3 us  [the longest x1 16.2 us: on_device(): pl.pallas_call(functools.partial(answer_kernel, kv), out_shape=messages,...]
    all_to_all x3 -> x1, starting transfers between devices: 16.4 us -> 3.81 us  [exchange(): boxed = lax.all_to_all(boxed, AXES, split_axis=0, concat_axis=0, tiled=True)]
    all_to_all x1, blocking collectives: 21.2 us -> 31.7 us  [exchange(): boxed = lax.all_to_all(boxed, AXES, split_axis=0, concat_axis=0, tiled=True)]
    unnamed x14 -> x22, local copies, waits for them, and re-layouts: 0.03 us -> 8.8 us
    dot_general x6 -> x0, matrix products: 7.08 us -> none  [the longest x1 2.87 us: page_partials(): jnp.einsum('mqd,mjd->mqj', query_tiles, got_keys, preferred_element_type=...]
    reduce_sum x5 -> x0, other arithmetic: 2.3 us -> none  [the longest x2 1.42 us: on_device(): local_sum = jnp.sum(near_weights, axis=3) + jnp.sum(fresh_weights, axis=3)]
  transfers between devices with their start and end apart: 3 -> 1, of which waited for: 3 -> 1; matrix products, arithmetic and copies ran while one was open for 16% -> 0% of each run, Pallas kernels for 0% -> 4%
where the time goes in v1:
time: 88.8 us; the launch traced here: 88.4 us
  blocking collectives  31.7 us (36%)
  Pallas kernels  25.3 us (28%)
  waiting for transfers between devices  17.1 us (19%)
  local copies, waits for them, and re-layouts  10.4 us (12%)
  starting transfers between devices  3.81 us (4%)
    all_to_all x1, blocking collectives, exchange(): boxed = lax.all_to_all(boxed, AXES, split_axis=0, concat_axis=0, tiled=True)  31.7 us
    all_to_all x1, waiting for transfers between devices, exchange(): boxed = lax.all_to_all(boxed, AXES, split_axis=0, concat_axis=0, tiled=True)  17.1 us
    pallas_call x1, Pallas kernels, on_device(): pl.pallas_call(functools.partial(answer_kernel, kv), out_shape=messages,...  16.2 us
    unnamed x22, local copies, waits for them, and re-layouts  8.8 us
    all_to_all x1, starting transfers between devices, exchange(): boxed = lax.all_to_all(boxed, AXES, split_axis=0, concat_axis=0, tiled=True)  3.81 us
    pallas_call x1, Pallas kernels, on_device(): pl.pallas_call(local_kernel, out_shape=(near, near), in_specs=[VMEM] * 5,...  3.49 us
    pallas_call x1, Pallas kernels, on_device(): pl.pallas_call(functools.partial(merge_kernel, picks), out_shape=jax.Shap...  3.37 us
    pallas_call x1, Pallas kernels, on_device(): pl.pallas_call(functools.partial(pack_kernel, picks), out_shape=(messages...  2.28 us
  transfers between devices with their start and end apart: 1, of which 1 were waited for; matrix products, arithmetic and copies ran while one was open for 0% of the time, Pallas kernels for 4%

profile of v1, /device:TPU:1, one launch (start us, length us, event | category | flops | bytes accessed | tf_op | source)
XLA Modules:
  0.0 88.4 jit_solution(4770220964919534071)
XLA Ops:
  0.0 0.8 reshape.24.owner
  0.8 0.8 reshape.25.slot
  1.6 0.0 copy-start.4
  1.6 0.8 copy-done.4
  2.4 2.3 %pack.1 = (bf16[4352,128]{1,0:T(8,128)(2,1)S(1)}, s32[128]{0:T(128)S(1)}) custom-call(s32[128]{0:T(128)S(1)} %reshape.24.owner, s32[128]{0:T(128)S(1)} %reshape.25.slot, bf16[2,2,8,1024]{3,2,1,0:T(8,128)(2,1)S(1)} %copy-done.4), custom_call_target="tpu_custom_call" | custom-call | tf_op jit(solution)/shard_map/pack/pallas_call | solution.py:283
  4.7 0.0 copy-start.9
  4.7 0.5 copy-done.9
  5.2 0.0 copy-start.8
  5.2 31.7 %all_to_all.10 = bf16[128,17,2,128]{3,2,1,0:T(2,128)(2,1)S(1)} all-to-all(bf16[128,17,2,128]{3,2,1,0:T(2,128)(2,1)S(1)} %bitcast.10), channel_id=1, replica_groups=mesh['ctx'=32,'rows'=4] {'ctx','rows'}, dimensions={0} | all-to-all | bytes 2228224 | tf_op jit(solution)/shard_map/all_to_all | solution.py:257
  37.0 0.0 copy-done.8
  37.0 0.0 copy-start
  37.0 3.4 %copy-done = bf16[64,8,64,128]{3,2,1,0:T(8,128)(2,1)S(1)} copy-done((bf16[64,8,64,128]{3,2,1,0:T(8,128)(2,1)S(1)}, bf16[64,8,64,128]{3,2,1,0:T(8,128)(2,1)}, u32[]{:S(2)}) %copy-start) | copy-done | bytes 8388632
  40.4 0.0 copy-start.1
  40.4 3.4 %copy-done.1 = bf16[64,8,64,128]{3,2,1,0:T(8,128)(2,1)S(1)} copy-done((bf16[64,8,64,128]{3,2,1,0:T(8,128)(2,1)S(1)}, bf16[64,8,64,128]{3,2,1,0:T(8,128)(2,1)}, u32[]{:S(2)}) %copy-start.1) | copy-done | bytes 8388632
  43.7 16.2 %answer.1 = bf16[4352,128]{1,0:T(8,128)(2,1)} custom-call(s32[64]{0:T(128)S(1)} %copy-done.8, bf16[4352,128]{1,0:T(8,128)(2,1)S(1)} %bitcast.8, bf16[512,64,128]{2,1,0:T(8,128)(2,1)S(1)} %bitcast.6, bf16[512,64,128]{2,1,0:T(8,128)(2,1)S(1)} %bitcast.7), custom_call_target="tpu_custom_call" | custom-call | tf_op jit(solution)/shard_map/answer/pallas_call | solution.py:308
  59.9 0.0 copy-start.2
  59.9 0.0 copy-start.3
  59.9 0.0 copy-start.5
  59.9 0.0 copy-start.6
  60.0 0.0 copy-start.7
  60.0 3.8 %all-to-all-start.1 = ((bf16[128,17,2,128]{3,2,1,0:T(2,128)(2,1)}), bf16[128,17,2,128]{3,2,1,0:T(2,128)(2,1)S(1)}, u32[]{:S(2)}, u32[]{:S(2)}) async-start(bf16[128,17,2,128]{3,2,1,0:T(2,128)(2,1)} %bitcast.4), calls=%async_computation.1 | async-start | bytes 2228224 | tf_op jit(solution)/shard_map/all_to_all | solution.py:257
  63.8 0.0 copy-done.2
  63.8 0.0 copy-done.3
  63.8 0.0 copy-done.5
  63.8 0.0 copy-done.6
  63.8 0.0 copy-done.7
  63.8 3.5 %near.1 = (f32[256,128]{1,0:T(8,128)S(1)}, f32[256,128]{1,0:T(8,128)S(1)}) custom-call(bf16[2,2,8,1024]{3,2,1,0:T(8,128)(2,1)S(1)} %copy-done.5, bf16[2,2,8,128]{3,2,1,0:T(8,128)(2,1)S(1)} %copy-done.6, bf16[2,2,8,128]{3,2,1,0:T(8,128)(2,1)S(1)} %copy-done.7, bf16[2,8,256,128]{3,2,1,0:T(8,128)(2,1)S(1)} %copy-done.2, bf16[2,8,256,128]{3,2,1,0:T(8,128)(2,1)S(1)} %copy-done.3), custom_call_target="tpu_custom_call" | custom-call | flops 70000000 | bytes 3000000 | tf_op jit(solution)/shard_map/near/pallas_call | solution.py:295
  67.3 17.1 %all-to-all-done.1 = bf16[128,17,2,128]{3,2,1,0:T(2,128)(2,1)S(1)} async-done(((bf16[128,17,2,128]{3,2,1,0:T(2,128)(2,1)}), bf16[128,17,2,128]{3,2,1,0:T(2,128)(2,1)S(1)}, u32[]{:S(2)}, u32[]{:S(2)}) %all-to-all-start.1) | async-done | bytes 1114144 | tf_op jit(solution)/shard_map/all_to_all | solution.py:257
  84.4 0.0 copy-start.10
  84.4 0.7 copy-done.10
  85.0 3.4 %merge.1 = bf16[2,2,8,1024]{3,2,1,0:T(8,128)(2,1)} custom-call(s32[128]{0:T(128)S(1)} %copy-done.10, bf16[4352,128]{1,0:T(8,128)(2,1)S(1)} %bitcast.9, f32[256,128]{1,0:T(8,128)S(1)} %get-tuple-element.11.mixed, f32[256,128]{1,0:T(8,128)S(1)} %get-tuple-element.12.level), custom_call_target="tpu_custom_call" | custom-call | tf_op jit(solution)/shard_map/merge/pallas_call | solution.py:330
Async XLA Ops:
  1.6 0.8 copy-start.4
  4.7 0.5 copy-start.9
  5.2 31.8 %copy-start.8 = (s32[64]{0:T(128)S(1)}, s32[64]{0:T(128)}, u32[]{:S(2)}) copy-start(s32[64]{0:T(128)} %fill.1) | copy-start | bytes 772
  37.0 3.4 %copy-start = (bf16[64,8,64,128]{3,2,1,0:T(8,128)(2,1)S(1)}, bf16[64,8,64,128]{3,2,1,0:T(8,128)(2,1)}, u32[]{:S(2)}) copy-start(bf16[64,8,64,128]{3,2,1,0:T(8,128)(2,1)} %param.15) | copy-start | bytes 25165828
  40.4 3.4 %copy-start.1 = (bf16[64,8,64,128]{3,2,1,0:T(8,128)(2,1)S(1)}, bf16[64,8,64,128]{3,2,1,0:T(8,128)(2,1)}, u32[]{:S(2)}) copy-start(bf16[64,8,64,128]{3,2,1,0:T(8,128)(2,1)} %param.16) | copy-start | bytes 25165828
  59.9 3.9 %copy-start.2 = (bf16[2,8,256,128]{3,2,1,0:T(8,128)(2,1)S(1)}, bf16[2,8,256,128]{3,2,1,0:T(8,128)(2,1)}, u32[]{:S(2)}) copy-start(bf16[2,8,256,128]{3,2,1,0:T(8,128)(2,1)} %keys.1) | copy-start | bytes 3145732
  59.9 3.9 %copy-start.3 = (bf16[2,8,256,128]{3,2,1,0:T(8,128)(2,1)S(1)}, bf16[2,8,256,128]{3,2,1,0:T(8,128)(2,1)}, u32[]{:S(2)}) copy-start(bf16[2,8,256,128]{3,2,1,0:T(8,128)(2,1)} %values.1) | copy-start | bytes 3145732
  59.9 3.9 %copy-start.5 = (bf16[2,2,8,1024]{3,2,1,0:T(8,128)(2,1)S(1)}, bf16[2,2,8,1024]{3,2,1,0:T(8,128)(2,1)}, u32[]{:S(2)}) copy-start(bf16[2,2,8,1024]{3,2,1,0:T(8,128)(2,1)} %queries.3) | copy-start | bytes 196612
  59.9 3.9 %copy-start.6 = (bf16[2,2,8,128]{3,2,1,0:T(8,128)(2,1)S(1)}, bf16[2,2,8,128]{3,2,1,0:T(8,128)(2,1)}, u32[]{:S(2)}) copy-start(bf16[2,2,8,128]{3,2,1,0:T(8,128)(2,1)} %new_keys.1) | copy-start | bytes 24580
  60.0 3.9 %copy-start.7 = (bf16[2,2,8,128]{3,2,1,0:T(8,128)(2,1)S(1)}, bf16[2,2,8,128]{3,2,1,0:T(8,128)(2,1)}, u32[]{:S(2)}) copy-start(bf16[2,2,8,128]{3,2,1,0:T(8,128)(2,1)} %new_values.1) | copy-start | bytes 24580
  60.0 24.4 %all-to-all-start.1 = ((bf16[128,17,2,128]{3,2,1,0:T(2,128)(2,1)}), bf16[128,17,2,128]{3,2,1,0:T(2,128)(2,1)S(1)}, u32[]{:S(2)}, u32[]{:S(2)}) async-start(bf16[128,17,2,128]{3,2,1,0:T(2,128)(2,1)} %bitcast.4), calls=%async_computation.1 | async-start | bytes 2228224 | tf_op jit(solution)/shard_map/all_to_all | solution.py:257
  84.4 0.7 copy-start.10

commit v2 on v1

v2 whole, which is shorter than its diff:
```python
import functools

import jax
import jax.numpy as jnp
from jax import lax
from jax.experimental import pallas as pl
from jax.experimental.pallas import tpu as pltpu
from jax.sharding import PartitionSpec as P

AXES = ("ctx", "rows")
FLOOR = -1e30
LANES = 128
SLOTS = 2
TILE = 16
SPAN = SLOTS * TILE + SLOTS
PIECES = 3
MIB = 1024 * 1024


def lane_iota(rows):
    return lax.broadcasted_iota(jnp.int32, (rows, LANES), 1)


def row_iota(rows):
    return lax.broadcasted_iota(jnp.int32, (rows, LANES), 0)


def load_tiles(queries, tiles):
    seqs, steps, kv, wide = queries.shape
    group = wide // LANES
    for s in range(seqs):
        for t in range(steps):
            for h in range(group):
                block = queries[s, t, :, h * LANES : (h + 1) * LANES]
                start = s * kv * TILE + t * group + h
                tiles[pl.ds(start, kv, stride=TILE), :] = block.astype(jnp.float32)


def pack_kernel(owner_hbm, slot_hbm, queries_hbm, out, place, owner, slot, queries, tiles, wide, count, sems):
    devices = wide.shape[0] // SPAN
    seqs, kv, picks = owner.shape
    copies = [
        pltpu.make_async_copy(source, target, sems.at[i])
        for i, (source, target) in enumerate(
            ((owner_hbm, owner), (slot_hbm, slot), (queries_hbm, queries))
        )
    ]
    for copy in copies:
        copy.start()
    wide[...] = jnp.zeros_like(wide)
    for i in range(devices):
        count[i] = 0
    for copy in copies:
        copy.wait()
    load_tiles(queries, tiles)
    lane = lane_iota(1)

    def fill_tiles(s, g):
        tile = s * kv + g
        block = tiles[pl.ds(pl.multiple_of(tile * TILE, TILE), TILE), :]
        to = [owner[s, g, k] for k in range(picks)]
        used = [count[d] for d in to]
        for k in range(picks):
            count[to[k]] = used[k] + 1
        for k in range(picks):
            base = to[k] * SPAN
            place[tile * picks + k] = to[k] * SLOTS + used[k]
            wide[pl.ds(base + used[k] * TILE, TILE), :] = block
            code = jnp.where(lane < LANES // 2, slot[s, g, k] + 1, g).astype(jnp.float32)
            wide[pl.ds(base + SLOTS * TILE + used[k], 1), :] = code

    for s in range(seqs):
        for g in range(kv):
            fill_tiles(s, g)
    out[...] = wide[...].astype(out.dtype)


def local_kernel(
    queries,
    new_keys,
    new_values,
    keys,
    values,
    mixed,
    level,
    tiles,
    fresh,
):
    seqs, steps, kv, wide = queries.shape
    group = wide // LANES
    recent = keys.shape[2]
    scale = LANES ** (-0.5)
    load_tiles(queries, tiles)
    news = seqs * steps * kv
    for s in range(seqs):
        for u in range(steps):
            at = (s * steps + u) * kv
            fresh[at : at + kv, :] = new_keys[s, u].astype(jnp.float32)
            fresh[news + at : news + at + kv, :] = new_values[s, u].astype(jnp.float32)
    fresh_keys = fresh[:news, :].astype(jnp.bfloat16)
    fresh_values = jnp.concatenate(
        [fresh[news:, :].astype(jnp.bfloat16), jnp.ones((news, LANES), jnp.bfloat16)], axis=1
    )
    ones = jnp.ones((recent, LANES), jnp.bfloat16)
    col = lax.broadcasted_iota(jnp.int32, (TILE, news), 1)
    step = lax.broadcasted_iota(jnp.int32, (TILE, news), 0) // group
    nt = (((1,), (1,)), ((), ()))
    for s in range(seqs):
        for g in range(kv):
            at = (s * kv + g) * TILE
            query = tiles[at : at + TILE, :].astype(jnp.bfloat16)
            near = lax.dot_general(query, keys[s, g], nt, preferred_element_type=jnp.float32) * scale
            late = lax.dot_general(query, fresh_keys, nt, preferred_element_type=jnp.float32) * scale
            first = s * steps * kv + g
            seen = (col >= first) & (col <= first + step * kv) & (lax.rem(col, kv) == g)
            late = jnp.where(seen, late, FLOOR)
            peak = jnp.maximum(
                jnp.max(near, axis=1, keepdims=True), jnp.max(late, axis=1, keepdims=True)
            )
            near_weights = jnp.exp(near - peak).astype(jnp.bfloat16)
            late_weights = jnp.exp(late - peak).astype(jnp.bfloat16)
            both = jnp.concatenate([values[s, g], ones], axis=1)
            total = lax.dot(near_weights, both, preferred_element_type=jnp.float32)
            total = total + lax.dot(late_weights, fresh_values, preferred_element_type=jnp.float32)
            weight = total[:, LANES:]
            mixed[at : at + TILE, :] = total[:, :LANES]
            level[at : at + TILE, :LANES] = jnp.broadcast_to(peak, (TILE, LANES))
            level[at : at + TILE, LANES:] = weight


def read_codes(pages, wide, codes):
    devices = wide.shape[0] // SPAN
    half = LANES // 2
    lane = lane_iota(1)
    rows = []
    heads = []
    for c in range(SLOTS):
        low = jnp.zeros((8, LANES), jnp.float32)
        high = jnp.zeros((8, LANES), jnp.float32)
        for j in range(devices // 8):
            start = j * 8 * SPAN + SLOTS * TILE + c
            block = wide[pl.ds(start, 8, stride=SPAN), :]
            mine = lax.rem(lane_iota(8), half) == lax.rem(row_iota(8) + j * 8, half)
            block = jnp.where(mine, block, 0.0)
            if j * 8 < half:
                low = low + block
            else:
                high = high + block
        low = jnp.sum(low, axis=0, keepdims=True)
        high = jnp.sum(high, axis=0, keepdims=True)
        row = jnp.where(lane < half, low, pltpu.roll(high, half, 1)).astype(jnp.int32)
        head = jnp.where(lane < half, pltpu.roll(low, half, 1), high).astype(jnp.int32)
        rows.append(jnp.where(row == 0, lax.rem(lane, pages), row - 1))
        heads.append(jnp.where(row == 0, lane // pages + c * (LANES // pages), head))
    spare = [jnp.zeros_like(rows[0])] * (codes.shape[0] - 2 * SLOTS)
    codes[...] = jnp.concatenate(rows + heads + spare, axis=0)


def answer_kernel(
    kv,
    batch,
    ahead,
    fill,
    got,
    keys,
    values,
    unused,
    out,
    wide,
    answer,
    sides,
    near_keys,
    near_values,
    codes_v,
    codes,
    sem,
    key_sems,
    value_sems,
):
    devices = wide.shape[0] // SPAN
    page = keys.shape[1]
    scale = LANES ** (-0.5)
    wide[...] = got[...].astype(jnp.float32)
    read_codes(fill.shape[0], wide, codes_v)
    copy = pltpu.make_async_copy(codes_v, codes, sem)
    copy.start()
    copy.wait()
    nt = (((1,), (1,)), ((), ()))
    lane = lane_iota(TILE)
    mine = lax.rem(lane, TILE) == row_iota(TILE)
    front = lane < PIECES * TILE
    per_score, per_mix = 4, 2
    ones = jnp.ones((per_mix * page, LANES), jnp.bfloat16)
    rounds = devices * SLOTS // batch

    def pull(step):
        for a in range(batch):
            item = step * batch + a
            where = codes[item % SLOTS, item // SLOTS] * kv + codes[SLOTS + item % SLOTS, item // SLOTS]
            pltpu.make_async_copy(keys.at[where], near_keys.at[item], key_sems.at[step]).start()
            pltpu.make_async_copy(values.at[where], near_values.at[item], value_sems.at[step]).start()

    def attend(step):
        span = pl.ds(step * batch, batch)
        pltpu.make_async_copy(keys.at[pl.ds(0, batch)], near_keys.at[span], key_sems.at[step]).wait()
        pltpu.make_async_copy(values.at[pl.ds(0, batch)], near_values.at[span], value_sems.at[step]).wait()
        spots, rows, fills, queries = [], [], [], []
        for a in range(batch):
            item = step * batch + a
            message, c = item // SLOTS, item % SLOTS
            spots.append(message * SPAN + c * TILE)
            rows.append(c * devices + message)
            fills.append(fill[codes[c, message]])
            queries.append(wide[pl.ds(spots[a], TILE), :].astype(jnp.bfloat16))
        scores = []
        for b in range(0, batch, per_score):
            block = lax.dot_general(
                jnp.concatenate(queries[b : b + per_score], axis=0),
                near_keys[pl.ds(step * batch + b, per_score)].reshape(per_score * page, LANES),
                nt,
                preferred_element_type=jnp.float32,
            )
            for a in range(per_score):
                column = a * page // LANES * LANES
                scores.append(block[a * TILE : (a + 1) * TILE, column : column + LANES])
        peaks, weights = [], []
        for a in range(batch):
            first = a * page % LANES
            live = (lane >= first) & (lane < first + fills[a])
            part = jnp.where(live, scores[a], FLOOR)
            peak = jnp.max(part, axis=1, keepdims=True)
            peaks.append(peak * scale)
            weights.append(jnp.exp((part - peak) * scale))
        totals = []
        for b in range(0, batch, per_mix):
            mix = jnp.concatenate(weights[b : b + per_mix], axis=0).astype(jnp.bfloat16)
            both = jnp.concatenate([near_values[pl.ds(step * batch + b, per_mix)].reshape(per_mix * page, LANES), ones], axis=1)
            block = lax.dot(mix, both, preferred_element_type=jnp.float32)
            for a in range(per_mix):
                totals.append(block[a * TILE : (a + 1) * TILE, :])
        for a in range(batch):
            answer[pl.ds(spots[a], TILE), :] = totals[a][:, :LANES]
            side = jnp.where(front, peaks[a], totals[a][:, LANES:])
            side = jnp.where(mine, side, 0.0)
            sides[pl.ds(rows[a], 1), :] = jnp.sum(side, axis=0, keepdims=True)

    for step in range(ahead):
        pull(step)
    for step in range(rounds):
        if step + ahead < rounds:
            pull(step + ahead)
        attend(step)
    piece = lax.rem(lane_iota(8) // TILE, PIECES)
    for c in range(SLOTS):
        for j in range(devices // 8):
            value = sides[c * devices + j * 8 : c * devices + j * 8 + 8, :]
            high = value.astype(jnp.bfloat16).astype(jnp.float32)
            rest = value - high
            middle = rest.astype(jnp.bfloat16).astype(jnp.float32)
            value = jnp.where(piece == 0, high, jnp.where(piece == 1, middle, rest - middle))
            answer[pl.ds(j * 8 * SPAN + SLOTS * TILE + c, 8, stride=SPAN), :] = value
    out[...] = answer[...].astype(out.dtype)


def merge_kernel(picks, batch, place, got, mixed, level, out, wide, merged):
    seqs, steps, kv, width = out.shape
    group = width // LANES
    wide[...] = got[...].astype(jnp.float32)
    lane = lane_iota(TILE)
    mine = (lax.rem(lane, TILE) == row_iota(TILE)) & (lane < 2 * PIECES * TILE)
    source = lax.broadcasted_iota(jnp.int32, (LANES, 2 * LANES), 0) // (PIECES * TILE)
    target = lax.broadcasted_iota(jnp.int32, (LANES, 2 * LANES), 1) // LANES
    spread = (source == target).astype(jnp.float32).astype(jnp.bfloat16)

    def merge(step, carry):
        spots, sums = [], []
        for b in range(batch):
            sides = []
            for k in range(picks):
                spot = place[(step * batch + b) * picks + k]
                message = spot // SLOTS
                c = lax.rem(spot, SLOTS)
                spots.append(message * SPAN + c * TILE)
                side = wide[pl.ds(message * SPAN + SLOTS * TILE + c, 1), :]
                sides.append(jnp.where(mine, side, 0.0))
            sides = jnp.concatenate(sides, axis=0).astype(jnp.bfloat16)
            sums.append(lax.dot(sides, spread, preferred_element_type=jnp.float32))
        for b in range(batch):
            at = pl.multiple_of((step * batch + b) * TILE, TILE)
            rows = [sums[b][k * TILE : (k + 1) * TILE, :] for k in range(picks)]
            rows.append(level[pl.ds(at, TILE), :])
            parts = [wide[pl.ds(spots[b * picks + k], TILE), :] for k in range(picks)]
            parts.append(mixed[pl.ds(at, TILE), :])
            peak = functools.reduce(jnp.maximum, [x[:, :LANES] for x in rows])
            shares = [jnp.exp(x[:, :LANES] - peak) for x in rows]
            total = functools.reduce(jnp.add, [w * x for w, x in zip(shares, parts)])
            weight = functools.reduce(jnp.add, [w * x[:, LANES:] for w, x in zip(shares, rows)])
            merged[pl.ds(at, TILE), :] = total / weight
        return carry

    lax.fori_loop(0, seqs * kv // batch, merge, 0)
    for s in range(seqs):
        for t in range(steps):
            for h in range(group):
                start = s * kv * TILE + t * group + h
                block = merged[pl.ds(start, kv, stride=TILE), :]
                out[s, t, :, h * LANES : (h + 1) * LANES] = block.astype(out.dtype)


VMEM = pl.BlockSpec(memory_space=pltpu.VMEM)
SMEM = pl.BlockSpec(memory_space=pltpu.SMEM)
ANY = pl.BlockSpec(memory_space=pl.ANY)


def params(limit):
    return pltpu.CompilerParams(vmem_limit_bytes=limit * MIB)


def in_hbm(array):
    return pltpu.with_memory_space_constraint(array, pltpu.HBM)


def exchange(messages, devices):
    boxed = messages.reshape(devices, SPAN // 2, 2, LANES)
    boxed = lax.all_to_all(boxed, AXES, split_axis=0, concat_axis=0, tiled=True)
    return boxed.reshape(devices * SPAN, LANES)


def on_device(
    queries,
    new_keys,
    new_values,
    recent_keys,
    recent_values,
    page_keys,
    page_values,
    page_fill,
    top_owner,
    top_slot,
):
    seqs, steps, kv, width = queries.shape
    picks = top_owner.shape[2]
    items = seqs * kv * picks
    devices = lax.axis_size(AXES)
    rows = devices * SPAN
    tile_rows = seqs * kv * TILE
    wide = pltpu.VMEM((rows, LANES), jnp.float32)
    tiles = pltpu.VMEM((tile_rows, LANES), jnp.float32)
    messages = jax.ShapeDtypeStruct((rows, LANES), jnp.bfloat16)

    asked, place = pl.pallas_call(
        pack_kernel,
        out_shape=(messages, jax.ShapeDtypeStruct((items,), jnp.int32)),
        in_specs=[ANY, ANY, ANY],
        out_specs=(VMEM, SMEM),
        scratch_shapes=[
            pltpu.SMEM(top_owner.shape, jnp.int32),
            pltpu.SMEM(top_slot.shape, jnp.int32),
            pltpu.VMEM(queries.shape, queries.dtype),
            tiles,
            wide,
            pltpu.SMEM((devices,), jnp.int32),
            pltpu.SemaphoreType.DMA((3,)),
        ],
        compiler_params=params(16),
        name="pack",
    )(in_hbm(top_owner), in_hbm(top_slot), in_hbm(queries))
    asked = exchange(asked, devices)

    mixed, level = pl.pallas_call(
        local_kernel,
        out_shape=(
            jax.ShapeDtypeStruct((tile_rows, LANES), jnp.float32),
            jax.ShapeDtypeStruct((tile_rows, 2 * LANES), jnp.float32),
        ),
        in_specs=[VMEM] * 5,
        out_specs=(VMEM,) * 2,
        scratch_shapes=[
            tiles,
            pltpu.VMEM((2 * seqs * steps * kv, LANES), jnp.float32),
        ],
        compiler_params=params(16),
        cost_estimate=pl.CostEstimate(flops=70_000_000, bytes_accessed=3_000_000, transcendentals=70_000),
        name="near",
    )(
        queries,
        new_keys,
        new_values,
        recent_keys,
        recent_values,
    )

    pool = (page_keys.shape[0] * kv, page_keys.shape[2], LANES)
    slots, batch = SLOTS * devices, 64
    pages = pltpu.VMEM((slots,) + pool[1:], page_keys.dtype)
    answers = pl.pallas_call(
        functools.partial(answer_kernel, kv, batch, 2),
        out_shape=messages,
        in_specs=[SMEM, VMEM, ANY, ANY, ANY],
        out_specs=VMEM,
        scratch_shapes=[
            wide,
            wide,
            pltpu.VMEM((slots, LANES), jnp.float32),
            pages,
            pages,
            pltpu.VMEM((8, LANES), jnp.int32),
            pltpu.SMEM((8, LANES), jnp.int32),
            pltpu.SemaphoreType.DMA,
            pltpu.SemaphoreType.DMA((slots // batch,)),
            pltpu.SemaphoreType.DMA((slots // batch,)),
        ],
        compiler_params=params(24),
        name="answer",
    )(page_fill, asked, in_hbm(page_keys.reshape(pool)), in_hbm(page_values.reshape(pool)), level)
    answers = exchange(answers, devices)

    return pl.pallas_call(
        functools.partial(merge_kernel, picks, 4),
        out_shape=jax.ShapeDtypeStruct(queries.shape, jnp.bfloat16),
        in_specs=[SMEM, VMEM, VMEM, VMEM],
        out_specs=VMEM,
        scratch_shapes=[wide, tiles],
        compiler_params=params(16),
        name="merge",
    )(place, answers, mixed, level)


def solution(mesh):
    split = P(AXES)
    return jax.shard_map(
        on_device,
        mesh=mesh,
        in_specs=(split,) * 10,
        out_specs=split,
        check_vma=False,
    )
```

time: 88.8 us -> 69.2 us (0.78)
  Pallas kernels: 25.3 us -> 15.8 us
  local copies, waits for them, and re-layouts: 10.4 us -> 1.86 us
  blocking collectives: 31.7 us -> 23.6 us
  starting transfers between devices: 3.81 us -> 11.5 us
  waiting for transfers between devices: 17.1 us -> 16.2 us
    pallas_call x4, Pallas kernels: 25.3 us -> 15.8 us  [the longest x1 6.74 us: on_device(): pl.pallas_call(functools.partial(answer_kernel, kv, batch, 2), out_shape=...]
    all_to_all x1, blocking collectives: 31.7 us -> 23.6 us  [exchange(): boxed = lax.all_to_all(boxed, AXES, split_axis=0, concat_axis=0, tiled=True)]
    all_to_all x1, starting transfers between devices: 3.81 us -> 11.5 us  [exchange(): boxed = lax.all_to_all(boxed, AXES, split_axis=0, concat_axis=0, tiled=True)]
    unnamed x22 -> x20, local copies, waits for them, and re-layouts: 8.8 us -> 1.86 us
    reshape x2 -> x0, local copies, waits for them, and re-layouts: 1.56 us -> none  [the longest x1 0.78 us: on_device(): top_slot.reshape(items)]
  transfers between devices with their start and end apart: 1 -> 1, of which waited for: 1 -> 1; matrix products, arithmetic and copies ran while one was open for 0% -> 0% of each run, Pallas kernels for 4% -> 5%
where the time goes in v2:
time: 69.2 us; the launch traced here: 69 us
  blocking collectives  23.6 us (34%)
  waiting for transfers between devices  16.2 us (23%)
  Pallas kernels  15.8 us (23%)
  starting transfers between devices  11.5 us (17%)
  local copies, waits for them, and re-layouts  1.86 us (3%)
    all_to_all x1, blocking collectives, exchange(): boxed = lax.all_to_all(boxed, AXES, split_axis=0, concat_axis=0, tiled=True)  23.6 us
    all_to_all x1, waiting for transfers between devices, exchange(): boxed = lax.all_to_all(boxed, AXES, split_axis=0, concat_axis=0, tiled=True)  16.2 us
    all_to_all x1, starting transfers between devices, exchange(): boxed = lax.all_to_all(boxed, AXES, split_axis=0, concat_axis=0, tiled=True)  11.5 us
    pallas_call x1, Pallas kernels, on_device(): pl.pallas_call(functools.partial(answer_kernel, kv, batch, 2), out_shape=...  6.74 us
    pallas_call x1, Pallas kernels, on_device(): pl.pallas_call(local_kernel, out_shape=(jax.ShapeDtypeStruct((tile_rows,...  3.49 us
    pallas_call x1, Pallas kernels, on_device(): pl.pallas_call(functools.partial(merge_kernel, picks, 4), out_shape=jax.S...  2.89 us
    pallas_call x1, Pallas kernels, on_device(): pl.pallas_call(pack_kernel, out_shape=(messages, jax.ShapeDtypeStruct((it...  2.65 us
    unnamed x20, local copies, waits for them, and re-layouts  1.86 us
  transfers between devices with their start and end apart: 1, of which 1 were waited for; matrix products, arithmetic and copies ran while one was open for 0% of the time, Pallas kernels for 5%

profile of v2, /device:TPU:1, one launch (start us, length us, event | category | flops | bytes accessed | tf_op | source)
XLA Modules:
  0.0 69.0 jit_solution(6852987907021629778)
XLA Ops:
  0.0 2.6 %pack.1 = (bf16[4352,128]{1,0:T(8,128)(2,1)}, s32[128]{0:T(128)S(1)}) custom-call(s32[2,8,8]{2,1,0:T(8,128)} %owner_hbm.1, s32[2,8,8]{2,1,0:T(8,128)} %slot_hbm.1, bf16[2,2,8,1024]{3,2,1,0:T(8,128)(2,1)} %queries.1), custom_call_target="tpu_custom_call" | custom-call | tf_op jit(solution)/shard_map/pack/pallas_call | solution.py:351
  2.7 0.0 copy-start.8
  2.7 0.5 copy-done.8
  3.2 0.0 copy-start
  3.2 0.0 copy-start.1
  3.2 0.0 copy-start.2
  3.2 0.0 copy-start.5
  3.2 0.0 copy-start.6
  3.2 11.5 %all-to-all-start = ((bf16[128,17,2,128]{3,2,1,0:T(2,128)(2,1)}), bf16[128,17,2,128]{3,2,1,0:T(2,128)(2,1)S(1)}, u32[]{:S(2)}, u32[]{:S(2)}) async-start(bf16[128,17,2,128]{3,2,1,0:T(2,128)(2,1)} %bitcast), calls=%async_computation | async-start | bytes 2228224 | tf_op jit(solution)/shard_map/all_to_all | solution.py:325
  14.7 0.0 copy-done
  14.7 0.0 copy-done.1
  14.7 0.0 copy-done.2
  14.7 0.0 copy-done.5
  14.7 0.0 copy-done.6
  14.8 3.5 %near.1 = (f32[256,128]{1,0:T(8,128)S(1)}, f32[256,256]{1,0:T(8,128)S(1)}) custom-call(bf16[2,2,8,1024]{3,2,1,0:T(8,128)(2,1)S(1)} %copy-done.2, bf16[2,2,8,128]{3,2,1,0:T(8,128)(2,1)S(1)} %copy-done.5, bf16[2,2,8,128]{3,2,1,0:T(8,128)(2,1)S(1)} %copy-done.6, bf16[2,8,256,128]{3,2,1,0:T(8,128)(2,1)S(1)} %copy-done, bf16[2,8,256,128]{3,2,1,0:T(8,128)(2,1)S(1)} %copy-done.1), custom_call_target="tpu_custom_call" | custom-call | flops 70000000 | bytes 3000000 | tf_op jit(solution)/shard_map/near/pallas_call | solution.py:370
  18.2 0.0 copy-start.3
  18.2 0.7 copy-done.3
  18.9 16.2 %all-to-all-done = bf16[128,17,2,128]{3,2,1,0:T(2,128)(2,1)S(1)} async-done(((bf16[128,17,2,128]{3,2,1,0:T(2,128)(2,1)}), bf16[128,17,2,128]{3,2,1,0:T(2,128)(2,1)S(1)}, u32[]{:S(2)}, u32[]{:S(2)}) %all-to-all-start) | async-done | bytes 1114144 | tf_op jit(solution)/shard_map/all_to_all | solution.py:325
  35.2 0.0 copy-start.7
  35.2 0.7 copy-done.7
  35.8 6.7 %answer.1 = bf16[4352,128]{1,0:T(8,128)(2,1)S(1)} custom-call(s32[64]{0:T(128)S(1)} %copy-done.7, bf16[4352,128]{1,0:T(8,128)(2,1)S(1)} %bitcast.6, bf16[512,64,128]{2,1,0:T(8,128)(2,1)} %bitcast.9, bf16[512,64,128]{2,1,0:T(8,128)(2,1)} %bitcast.10, f32[256,256]{1,0:T(8,128)S(1)} %get-tuple-element.11.unused.level), custom_call_target="tpu_custom_call" | custom-call | tf_op jit(solution)/shard_map/answer/pallas_call | solution.py:396
  42.6 0.0 copy-start.4
  42.6 0.0 copy-start.9
  42.6 23.6 %all_to_all.10 = bf16[128,17,2,128]{3,2,1,0:T(2,128)(2,1)S(1)} all-to-all(bf16[128,17,2,128]{3,2,1,0:T(2,128)(2,1)S(1)} %bitcast.7), channel_id=1, replica_groups=mesh['ctx'=32,'rows'=4] {'ctx','rows'}, dimensions={0} | all-to-all | bytes 2228224 | tf_op jit(solution)/shard_map/all_to_all | solution.py:325
  66.2 0.0 copy-done.4
  66.2 0.0 copy-done.9
  66.2 2.9 %merge.1 = bf16[2,2,8,1024]{3,2,1,0:T(8,128)(2,1)} custom-call(s32[128]{0:T(128)S(1)} %copy-done.9, bf16[4352,128]{1,0:T(8,128)(2,1)S(1)} %bitcast.8, f32[256,128]{1,0:T(8,128)S(1)} %copy-done.4, f32[256,256]{1,0:T(8,128)S(1)} %get-tuple-element.11.unused.level), custom_call_target="tpu_custom_call" | custom-call | tf_op jit(solution)/shard_map/merge/pallas_call | solution.py:418
Async XLA Ops:
  2.7 0.5 copy-start.8
  3.2 11.5 %copy-start = (bf16[2,8,256,128]{3,2,1,0:T(8,128)(2,1)S(1)}, bf16[2,8,256,128]{3,2,1,0:T(8,128)(2,1)}, u32[]{:S(2)}) copy-start(bf16[2,8,256,128]{3,2,1,0:T(8,128)(2,1)} %keys.1) | copy-start | bytes 3145732
  3.2 11.5 %copy-start.1 = (bf16[2,8,256,128]{3,2,1,0:T(8,128)(2,1)S(1)}, bf16[2,8,256,128]{3,2,1,0:T(8,128)(2,1)}, u32[]{:S(2)}) copy-start(bf16[2,8,256,128]{3,2,1,0:T(8,128)(2,1)} %values.1) | copy-start | bytes 3145732
  3.2 11.6 %copy-start.2 = (bf16[2,2,8,1024]{3,2,1,0:T(8,128)(2,1)S(1)}, bf16[2,2,8,1024]{3,2,1,0:T(8,128)(2,1)}, u32[]{:S(2)}) copy-start(bf16[2,2,8,1024]{3,2,1,0:T(8,128)(2,1)} %queries.1) | copy-start | bytes 196612
  3.2 11.6 %copy-start.5 = (bf16[2,2,8,128]{3,2,1,0:T(8,128)(2,1)S(1)}, bf16[2,2,8,128]{3,2,1,0:T(8,128)(2,1)}, u32[]{:S(2)}) copy-start(bf16[2,2,8,128]{3,2,1,0:T(8,128)(2,1)} %new_keys.1) | copy-start | bytes 24580
  3.2 11.6 %copy-start.6 = (bf16[2,2,8,128]{3,2,1,0:T(8,128)(2,1)S(1)}, bf16[2,2,8,128]{3,2,1,0:T(8,128)(2,1)}, u32[]{:S(2)}) copy-start(bf16[2,2,8,128]{3,2,1,0:T(8,128)(2,1)} %new_values.1) | copy-start | bytes 24580
  3.2 32.0 %all-to-all-start = ((bf16[128,17,2,128]{3,2,1,0:T(2,128)(2,1)}), bf16[128,17,2,128]{3,2,1,0:T(2,128)(2,1)S(1)}, u32[]{:S(2)}, u32[]{:S(2)}) async-start(bf16[128,17,2,128]{3,2,1,0:T(2,128)(2,1)} %bitcast), calls=%async_computation | async-start | bytes 2228224 | tf_op jit(solution)/shard_map/all_to_all | solution.py:325
  18.2 0.7 copy-start.3
  35.2 0.7 copy-start.7
  42.6 23.6 %copy-start.4 = (f32[256,128]{1,0:T(8,128)S(1)}, f32[256,128]{1,0:T(8,128)}, u32[]{:S(2)}) copy-start(f32[256,128]{1,0:T(8,128)} %copy-done.3) | copy-start | bytes 393220
  42.6 23.6 %copy-start.9 = (s32[128]{0:T(128)S(1)}, s32[128]{0:T(128)}, u32[]{:S(2)}) copy-start(s32[128]{0:T(128)} %copy-done.8) | copy-start | bytes 1540

commit v3 on v2

--- a/solution.py
+++ b/solution.py
@@ -36,7 +36,7 @@
                 tiles[pl.ds(start, kv, stride=TILE), :] = block.astype(jnp.float32)
 
 
-def pack_kernel(owner_hbm, slot_hbm, queries_hbm, out, place, owner, slot, queries, tiles, wide, count, sems):
+def pack_kernel(owner_hbm, slot_hbm, queries_hbm, out, owner, slot, queries, tiles, wide, narrow, count, sems):
     devices = wide.shape[0] // SPAN
     seqs, kv, picks = owner.shape
     copies = [
@@ -54,25 +54,43 @@
         copy.wait()
     load_tiles(queries, tiles)
     lane = lane_iota(1)
-
-    def fill_tiles(s, g):
-        tile = s * kv + g
-        block = tiles[pl.ds(pl.multiple_of(tile * TILE, TILE), TILE), :]
-        to = [owner[s, g, k] for k in range(picks)]
-        used = [count[d] for d in to]
-        for k in range(picks):
-            count[to[k]] = used[k] + 1
-        for k in range(picks):
-            base = to[k] * SPAN
-            place[tile * picks + k] = to[k] * SLOTS + used[k]
-            wide[pl.ds(base + used[k] * TILE, TILE), :] = block
-            code = jnp.where(lane < LANES // 2, slot[s, g, k] + 1, g).astype(jnp.float32)
-            wide[pl.ds(base + SLOTS * TILE + used[k], 1), :] = code
-
     for s in range(seqs):
         for g in range(kv):
-            fill_tiles(s, g)
-    out[...] = wide[...].astype(out.dtype)
+            tile = s * kv + g
+            block = tiles[tile * TILE : (tile + 1) * TILE, :]
+            to = [owner[s, g, k] for k in range(picks)]
+            used = [count[d] for d in to]
+            for k in range(picks):
+                count[to[k]] = used[k] + 1
+            for k in range(picks):
+                base = to[k] * SPAN
+                wide[pl.ds(base + used[k] * TILE, TILE), :] = block
+                code = jnp.where(lane < LANES // 2, slot[s, g, k] + 1, g).astype(jnp.float32)
+                wide[pl.ds(base + SLOTS * TILE + used[k], 1), :] = code
+    parts = narrow.shape[0]
+    rows = narrow.shape[1]
+    copies = []
+    for i in range(parts):
+        narrow[i] = wide[i * rows : (i + 1) * rows, :].astype(narrow.dtype)
+        copies.append(
+            pltpu.make_async_copy(narrow.at[i], out.at[pl.ds(i * rows, rows)], sems.at[3 + i])
+        )
+        copies[-1].start()
+    for copy in copies:
+        copy.wait()
+
+
+def place_items(owner, place, count):
+    seqs, kv, picks = owner.shape
+    for i in range(count.shape[0]):
+        count[i] = 0
+    for s in range(seqs):
+        for g in range(kv):
+            to = [owner[s, g, k] for k in range(picks)]
+            used = [count[d] for d in to]
+            for k in range(picks):
+                count[to[k]] = used[k] + 1
+                place[(s * kv + g) * picks + k] = to[k] * SLOTS + used[k]
 
 
 def local_kernel(
@@ -81,11 +99,18 @@
     new_values,
     keys,
     values,
+    owner_hbm,
     mixed,
     level,
+    place,
     tiles,
     fresh,
+    owner,
+    count,
+    sem,
 ):
+    copy = pltpu.make_async_copy(owner_hbm, owner, sem)
+    copy.start()
     seqs, steps, kv, wide = queries.shape
     group = wide // LANES
     recent = keys.shape[2]
@@ -126,28 +151,34 @@
             mixed[at : at + TILE, :] = total[:, :LANES]
             level[at : at + TILE, :LANES] = jnp.broadcast_to(peak, (TILE, LANES))
             level[at : at + TILE, LANES:] = weight
-
-
-def read_codes(pages, wide, codes):
-    devices = wide.shape[0] // SPAN
+    copy.wait()
+    place_items(owner, place, count)
+
+
+def read_codes(pages, got, codes):
+    devices = got.shape[0] // SPAN
     half = LANES // 2
     lane = lane_iota(1)
+    number = lax.rem(lane_iota(8), half)
+    sums = [[jnp.zeros((1, LANES), jnp.float32)] * 2 for _ in range(SLOTS)]
+    for k in range(8):
+        at = k * SPAN + SLOTS * TILE
+        low = at // TILE * TILE
+        inside = (at - low) // 8 * 8
+        part = [jnp.zeros((8, LANES), jnp.float32)] * 2
+        for j in range(devices // 8):
+            message = j * 8 + k
+            block = got[j * 8 * SPAN + low : j * 8 * SPAN + low + TILE, :].astype(jnp.float32)
+            block = jnp.where(number == message % half, block[inside : inside + 8, :], 0.0)
+            part[message // half] = part[message // half] + block
+        row = at - low - inside
+        for c in range(SLOTS):
+            for i in range(2):
+                sums[c][i] = sums[c][i] + part[i][row + c : row + c + 1, :]
     rows = []
     heads = []
     for c in range(SLOTS):
-        low = jnp.zeros((8, LANES), jnp.float32)
-        high = jnp.zeros((8, LANES), jnp.float32)
-        for j in range(devices // 8):
-            start = j * 8 * SPAN + SLOTS * TILE + c
-            block = wide[pl.ds(start, 8, stride=SPAN), :]
-            mine = lax.rem(lane_iota(8), half) == lax.rem(row_iota(8) + j * 8, half)
-            block = jnp.where(mine, block, 0.0)
-            if j * 8 < half:
-                low = low + block
-            else:
-                high = high + block
-        low = jnp.sum(low, axis=0, keepdims=True)
-        high = jnp.sum(high, axis=0, keepdims=True)
+        low, high = sums[c]
         row = jnp.where(lane < half, low, pltpu.roll(high, half, 1)).astype(jnp.int32)
         head = jnp.where(lane < half, pltpu.roll(low, half, 1), high).astype(jnp.int32)
         rows.append(jnp.where(row == 0, lax.rem(lane, pages), row - 1))
@@ -160,7 +191,7 @@
     kv,
     batch,
     ahead,
-    fill,
+    fill_hbm,
     got,
     keys,
     values,
@@ -173,18 +204,22 @@
     near_values,
     codes_v,
     codes,
-    sem,
+    fill,
+    sems,
     key_sems,
     value_sems,
 ):
     devices = wide.shape[0] // SPAN
     page = keys.shape[1]
     scale = LANES ** (-0.5)
+    fill_copy = pltpu.make_async_copy(fill_hbm, fill, sems.at[0])
+    fill_copy.start()
+    read_codes(fill.shape[0], got, codes_v)
+    codes_copy = pltpu.make_async_copy(codes_v, codes, sems.at[1])
+    codes_copy.start()
     wide[...] = got[...].astype(jnp.float32)
-    read_codes(fill.shape[0], wide, codes_v)
-    copy = pltpu.make_async_copy(codes_v, codes, sem)
-    copy.start()
-    copy.wait()
+    fill_copy.wait()
+    codes_copy.wait()
     nt = (((1,), (1,)), ((), ()))
     lane = lane_iota(TILE)
     mine = lax.rem(lane, TILE) == row_iota(TILE)
@@ -192,6 +227,7 @@
     per_score, per_mix = 4, 2
     ones = jnp.ones((per_mix * page, LANES), jnp.bfloat16)
     rounds = devices * SLOTS // batch
+    piece = lax.rem(lane_iota(8) // TILE, PIECES)
 
     def pull(step):
         for a in range(batch):
@@ -209,7 +245,7 @@
             item = step * batch + a
             message, c = item // SLOTS, item % SLOTS
             spots.append(message * SPAN + c * TILE)
-            rows.append(c * devices + message)
+            rows.append(c * (batch // SLOTS) + a // SLOTS)
             fills.append(fill[codes[c, message]])
             queries.append(wide[pl.ds(spots[a], TILE), :].astype(jnp.bfloat16))
         scores = []
@@ -243,6 +279,18 @@
             side = jnp.where(front, peaks[a], totals[a][:, LANES:])
             side = jnp.where(mine, side, 0.0)
             sides[pl.ds(rows[a], 1), :] = jnp.sum(side, axis=0, keepdims=True)
+        for c in range(SLOTS):
+            for j in range(0, batch // SLOTS, 8):
+                first = c * (batch // SLOTS) + j
+                value = sides[first : first + 8, :]
+                high = value.astype(jnp.bfloat16).astype(jnp.float32)
+                rest = value - high
+                middle = rest.astype(jnp.bfloat16).astype(jnp.float32)
+                value = jnp.where(piece == 0, high, jnp.where(piece == 1, middle, rest - middle))
+                start = (step * (batch // SLOTS) + j) * SPAN + SLOTS * TILE + c
+                answer[pl.ds(start, 8, stride=SPAN), :] = value
+        span = pl.ds(step * (batch // SLOTS) * SPAN, batch // SLOTS * SPAN)
+        out[span, :] = answer[span, :].astype(out.dtype)
 
     for step in range(ahead):
         pull(step)
@@ -250,29 +298,22 @@
         if step + ahead < rounds:
             pull(step + ahead)
         attend(step)
-    piece = lax.rem(lane_iota(8) // TILE, PIECES)
-    for c in range(SLOTS):
-        for j in range(devices // 8):
-            value = sides[c * devices + j * 8 : c * devices + j * 8 + 8, :]
-            high = value.astype(jnp.bfloat16).astype(jnp.float32)
-            rest = value - high
-            middle = rest.astype(jnp.bfloat16).astype(jnp.float32)
-            value = jnp.where(piece == 0, high, jnp.where(piece == 1, middle, rest - middle))
-            answer[pl.ds(j * 8 * SPAN + SLOTS * TILE + c, 8, stride=SPAN), :] = value
-    out[...] = answer[...].astype(out.dtype)
-
-
-def merge_kernel(picks, batch, place, got, mixed, level, out, wide, merged):
+
+
+def merge_kernel(picks, batch, place_hbm, got, mixed, level, out, wide, merged, place, sem):
     seqs, steps, kv, width = out.shape
     group = width // LANES
+    copy = pltpu.make_async_copy(place_hbm, place, sem)
+    copy.start()
     wide[...] = got[...].astype(jnp.float32)
+    copy.wait()
     lane = lane_iota(TILE)
     mine = (lax.rem(lane, TILE) == row_iota(TILE)) & (lane < 2 * PIECES * TILE)
     source = lax.broadcasted_iota(jnp.int32, (LANES, 2 * LANES), 0) // (PIECES * TILE)
     target = lax.broadcasted_iota(jnp.int32, (LANES, 2 * LANES), 1) // LANES
     spread = (source == target).astype(jnp.float32).astype(jnp.bfloat16)
 
-    def merge(step, carry):
+    def merge(step):
         spots, sums = [], []
         for b in range(batch):
             sides = []
@@ -286,7 +327,7 @@
             sides = jnp.concatenate(sides, axis=0).astype(jnp.bfloat16)
             sums.append(lax.dot(sides, spread, preferred_element_type=jnp.float32))
         for b in range(batch):
-            at = pl.multiple_of((step * batch + b) * TILE, TILE)
+            at = (step * batch + b) * TILE
             rows = [sums[b][k * TILE : (k + 1) * TILE, :] for k in range(picks)]
             rows.append(level[pl.ds(at, TILE), :])
             parts = [wide[pl.ds(spots[b * picks + k], TILE), :] for k in range(picks)]
@@ -296,9 +337,9 @@
             total = functools.reduce(jnp.add, [w * x for w, x in zip(shares, parts)])
             weight = functools.reduce(jnp.add, [w * x[:, LANES:] for w, x in zip(shares, rows)])
             merged[pl.ds(at, TILE), :] = total / weight
-        return carry
-
-    lax.fori_loop(0, seqs * kv // batch, merge, 0)
+
+    for step in range(seqs * kv // batch):
+        merge(step)
     for s in range(seqs):
         for t in range(steps):
             for h in range(group):
@@ -348,36 +389,42 @@
     tiles = pltpu.VMEM((tile_rows, LANES), jnp.float32)
     messages = jax.ShapeDtypeStruct((rows, LANES), jnp.bfloat16)
 
-    asked, place = pl.pallas_call(
+    parts = 4
+    asked = pl.pallas_call(
         pack_kernel,
-        out_shape=(messages, jax.ShapeDtypeStruct((items,), jnp.int32)),
+        out_shape=pltpu.HBM(messages.shape, messages.dtype),
         in_specs=[ANY, ANY, ANY],
-        out_specs=(VMEM, SMEM),
+        out_specs=ANY,
         scratch_shapes=[
             pltpu.SMEM(top_owner.shape, jnp.int32),
             pltpu.SMEM(top_slot.shape, jnp.int32),
             pltpu.VMEM(queries.shape, queries.dtype),
             tiles,
             wide,
+            pltpu.VMEM((parts, rows // parts, LANES), messages.dtype),
             pltpu.SMEM((devices,), jnp.int32),
-            pltpu.SemaphoreType.DMA((3,)),
+            pltpu.SemaphoreType.DMA((3 + parts,)),
         ],
         compiler_params=params(16),
         name="pack",
     )(in_hbm(top_owner), in_hbm(top_slot), in_hbm(queries))
     asked = exchange(asked, devices)
 
-    mixed, level = pl.pallas_call(
+    mixed, level, place = pl.pallas_call(
         local_kernel,
         out_shape=(
             jax.ShapeDtypeStruct((tile_rows, LANES), jnp.float32),
             jax.ShapeDtypeStruct((tile_rows, 2 * LANES), jnp.float32),
+            jax.ShapeDtypeStruct((items,), jnp.int32),
         ),
-        in_specs=[VMEM] * 5,
-        out_specs=(VMEM,) * 2,
+        in_specs=[VMEM] * 5 + [ANY],
+        out_specs=(VMEM, VMEM, SMEM),
         scratch_shapes=[
             tiles,
             pltpu.VMEM((2 * seqs * steps * kv, LANES), jnp.float32),
+            pltpu.SMEM(top_owner.shape, jnp.int32),
+            pltpu.SMEM((devices,), jnp.int32),
+            pltpu.SemaphoreType.DMA,
         ],
         compiler_params=params(16),
         cost_estimate=pl.CostEstimate(flops=70_000_000, bytes_accessed=3_000_000, transcendentals=70_000),
@@ -388,6 +435,7 @@
         new_values,
         recent_keys,
         recent_values,
+        in_hbm(top_owner),
     )
 
     pool = (page_keys.shape[0] * kv, page_keys.shape[2], LANES)
@@ -396,31 +444,37 @@
     answers = pl.pallas_call(
         functools.partial(answer_kernel, kv, batch, 2),
         out_shape=messages,
-        in_specs=[SMEM, VMEM, ANY, ANY, ANY],
+        in_specs=[ANY, VMEM, ANY, ANY, ANY],
         out_specs=VMEM,
         scratch_shapes=[
             wide,
             wide,
-            pltpu.VMEM((slots, LANES), jnp.float32),
+            pltpu.VMEM((batch, LANES), jnp.float32),
             pages,
             pages,
             pltpu.VMEM((8, LANES), jnp.int32),
             pltpu.SMEM((8, LANES), jnp.int32),
-            pltpu.SemaphoreType.DMA,
+            pltpu.SMEM(page_fill.shape, jnp.int32),
+            pltpu.SemaphoreType.DMA((2,)),
             pltpu.SemaphoreType.DMA((slots // batch,)),
             pltpu.SemaphoreType.DMA((slots // batch,)),
         ],
         compiler_params=params(24),
         name="answer",
-    )(page_fill, asked, in_hbm(page_keys.reshape(pool)), in_hbm(page_values.reshape(pool)), level)
+    )(in_hbm(page_fill), asked, in_hbm(page_keys.reshape(pool)), in_hbm(page_values.reshape(pool)), level)
     answers = exchange(answers, devices)
 
     return pl.pallas_call(
-        functools.partial(merge_kernel, picks, 4),
+        functools.partial(merge_kernel, picks, 8),
         out_shape=jax.ShapeDtypeStruct(queries.shape, jnp.bfloat16),
-        in_specs=[SMEM, VMEM, VMEM, VMEM],
+        in_specs=[ANY, VMEM, VMEM, VMEM],
         out_specs=VMEM,
-        scratch_shapes=[wide, tiles],
+        scratch_shapes=[
+            wide,
+            tiles,
+            pltpu.SMEM((items,), jnp.int32),
+            pltpu.SemaphoreType.DMA,
+        ],
         compiler_params=params(16),
         name="merge",
     )(place, answers, mixed, level)

time: 69.2 us -> 66.9 us (0.967)
  waiting for transfers between devices: 16.2 us -> 14.7 us
    all_to_all x1, waiting for transfers between devices: 16.2 us -> 14.7 us  [exchange(): boxed = lax.all_to_all(boxed, AXES, split_axis=0, concat_axis=0, tiled=True)]
    pallas_call x1, Pallas kernels: 3.49 us -> 4.49 us  [on_device(): pl.pallas_call(local_kernel, out_shape=(jax.ShapeDtypeStruct((tile_rows,...]
    pallas_call x2, Pallas kernels: 5.53 us -> 4.76 us  [the longest x1 2.48 us: on_device(): pl.pallas_call(pack_kernel, out_shape=pltpu.HBM(messages.shape, messages....]
    pallas_call x1, Pallas kernels: 6.74 us -> 6.01 us  [on_device(): pl.pallas_call(functools.partial(answer_kernel, kv, batch, 2), out_shape=...]
    unnamed x20 -> x18, local copies, waits for them, and re-layouts: 1.86 us -> 1.19 us
  transfers between devices with their start and end apart: 1 -> 1, of which waited for: 1 -> 1; matrix products, arithmetic and copies ran while one was open for 0% -> 0% of each run, Pallas kernels for 5% -> 7%
where the time goes in v3:
time: 66.9 us; the launch traced here: 66.6 us
  blocking collectives  23.8 us (36%)
  Pallas kernels  15.3 us (23%)
  waiting for transfers between devices  14.7 us (22%)
  starting transfers between devices  11.5 us (17%)
  local copies, waits for them, and re-layouts  1.19 us (2%)
    all_to_all x1, blocking collectives, exchange(): boxed = lax.all_to_all(boxed, AXES, split_axis=0, concat_axis=0, tiled=True)  23.8 us
    all_to_all x1, waiting for transfers between devices, exchange(): boxed = lax.all_to_all(boxed, AXES, split_axis=0, concat_axis=0, tiled=True)  14.7 us
    all_to_all x1, starting transfers between devices, exchange(): boxed = lax.all_to_all(boxed, AXES, split_axis=0, concat_axis=0, tiled=True)  11.5 us
    pallas_call x1, Pallas kernels, on_device(): pl.pallas_call(functools.partial(answer_kernel, kv, batch, 2), out_shape=...  6.01 us
    pallas_call x1, Pallas kernels, on_device(): pl.pallas_call(local_kernel, out_shape=(jax.ShapeDtypeStruct((tile_rows,...  4.49 us
    pallas_call x1, Pallas kernels, on_device(): pl.pallas_call(pack_kernel, out_shape=pltpu.HBM(messages.shape, messages....  2.48 us
    pallas_call x1, Pallas kernels, on_device(): pl.pallas_call(functools.partial(merge_kernel, picks, 8), out_shape=jax.S...  2.28 us
  transfers between devices with their start and end apart: 1, of which 1 were waited for; matrix products, arithmetic and copies ran while one was open for 0% of the time, Pallas kernels for 7%

profile of v3, /device:TPU:1, one launch (start us, length us, event | category | flops | bytes accessed | tf_op | source)
XLA Modules:
  0.0 66.6 jit_solution(7071588575573163644)
XLA Ops:
  0.0 2.5 %pack.1 = bf16[4352,128]{1,0:T(8,128)(2,1)} custom-call(s32[2,8,8]{2,1,0:T(8,128)} %owner_hbm.3, s32[2,8,8]{2,1,0:T(8,128)} %slot_hbm.1, bf16[2,2,8,1024]{3,2,1,0:T(8,128)(2,1)} %queries_hbm.1), custom_call_target="tpu_custom_call" | custom-call | tf_op jit(solution)/shard_map/pack/pallas_call | solution.py:393
  2.5 0.0 copy-start
  2.5 0.0 copy-start.1
  2.5 0.0 copy-start.2
  2.5 0.0 copy-start.5
  2.5 0.0 copy-start.6
  2.6 11.5 %all-to-all-start = ((bf16[128,17,2,128]{3,2,1,0:T(2,128)(2,1)}), bf16[128,17,2,128]{3,2,1,0:T(2,128)(2,1)S(1)}, u32[]{:S(2)}, u32[]{:S(2)}) async-start(bf16[128,17,2,128]{3,2,1,0:T(2,128)(2,1)} %bitcast.11), calls=%async_computation | async-start | bytes 2228224 | tf_op jit(solution)/shard_map/all_to_all | solution.py:366
  14.1 0.0 copy-done
  14.1 0.0 copy-done.1
  14.1 0.0 copy-done.2
  14.1 0.0 copy-done.5
  14.1 0.0 copy-done.6
  14.1 4.5 %near.1 = (f32[256,128]{1,0:T(8,128)S(1)}, f32[256,256]{1,0:T(8,128)S(1)}, s32[128]{0:T(128)S(1)}) custom-call(bf16[2,2,8,1024]{3,2,1,0:T(8,128)(2,1)S(1)} %copy-done.2, bf16[2,2,8,128]{3,2,1,0:T(8,128)(2,1)S(1)} %copy-done.5, bf16[2,2,8,128]{3,2,1,0:T(8,128)(2,1)S(1)} %copy-done.6, bf16[2,8,256,128]{3,2,1,0:T(8,128)(2,1)S(1)} %copy-done, ...), custom_call_target="tpu_custom_call" | custom-call | flops 70000000 | bytes 3000000 | tf_op jit(solution)/shard_map/near/pallas_call | solution.py:413
  18.6 0.0 copy-start.3
  18.6 0.6 copy-done.3
  19.3 0.0 copy-start.7
  19.3 0.5 copy-done.7
  19.8 14.7 %all-to-all-done = bf16[128,17,2,128]{3,2,1,0:T(2,128)(2,1)S(1)} async-done(((bf16[128,17,2,128]{3,2,1,0:T(2,128)(2,1)}), bf16[128,17,2,128]{3,2,1,0:T(2,128)(2,1)S(1)}, u32[]{:S(2)}, u32[]{:S(2)}) %all-to-all-start) | async-done | bytes 1114144 | tf_op jit(solution)/shard_map/all_to_all | solution.py:366
  34.5 6.0 %answer.1 = bf16[4352,128]{1,0:T(8,128)(2,1)S(1)} custom-call(s32[64]{0:T(128)} %fill_hbm.1, bf16[4352,128]{1,0:T(8,128)(2,1)S(1)} %bitcast.6, bf16[512,64,128]{2,1,0:T(8,128)(2,1)} %bitcast.9, bf16[512,64,128]{2,1,0:T(8,128)(2,1)} %bitcast.10, f32[256,256]{1,0:T(8,128)S(1)} %get-tuple-element.9.unused.level), custom_call_target="tpu_custom_call" | custom-call | tf_op jit(solution)/shard_map/answer/pallas_call | solution.py:444
  40.5 0.0 copy-start.4
  40.5 0.0 copy-start.8
  40.6 23.8 %all_to_all.10 = bf16[128,17,2,128]{3,2,1,0:T(2,128)(2,1)S(1)} all-to-all(bf16[128,17,2,128]{3,2,1,0:T(2,128)(2,1)S(1)} %bitcast.7), channel_id=1, replica_groups=mesh['ctx'=32,'rows'=4] {'ctx','rows'}, dimensions={0} | all-to-all | bytes 2228224 | tf_op jit(solution)/shard_map/all_to_all | solution.py:366
  64.3 0.0 copy-done.4
  64.4 0.0 copy-done.8
  64.4 2.3 %merge.1 = bf16[2,2,8,1024]{3,2,1,0:T(8,128)(2,1)} custom-call(s32[128]{0:T(128)S(1)} %copy-done.8, bf16[4352,128]{1,0:T(8,128)(2,1)S(1)} %bitcast.8, f32[256,128]{1,0:T(8,128)S(1)} %copy-done.4, f32[256,256]{1,0:T(8,128)S(1)} %get-tuple-element.9.unused.level), custom_call_target="tpu_custom_call" | custom-call | tf_op jit(solution)/shard_map/merge/pallas_call | solution.py:467
Async XLA Ops:
  2.5 11.6 %copy-start = (bf16[2,8,256,128]{3,2,1,0:T(8,128)(2,1)S(1)}, bf16[2,8,256,128]{3,2,1,0:T(8,128)(2,1)}, u32[]{:S(2)}) copy-start(bf16[2,8,256,128]{3,2,1,0:T(8,128)(2,1)} %keys.1) | copy-start | bytes 3145732
  2.5 11.6 %copy-start.1 = (bf16[2,8,256,128]{3,2,1,0:T(8,128)(2,1)S(1)}, bf16[2,8,256,128]{3,2,1,0:T(8,128)(2,1)}, u32[]{:S(2)}) copy-start(bf16[2,8,256,128]{3,2,1,0:T(8,128)(2,1)} %values.1) | copy-start | bytes 3145732
  2.5 11.6 %copy-start.2 = (bf16[2,2,8,1024]{3,2,1,0:T(8,128)(2,1)S(1)}, bf16[2,2,8,1024]{3,2,1,0:T(8,128)(2,1)}, u32[]{:S(2)}) copy-start(bf16[2,2,8,1024]{3,2,1,0:T(8,128)(2,1)} %queries_hbm.1) | copy-start | bytes 196612
  2.5 11.6 %copy-start.5 = (bf16[2,2,8,128]{3,2,1,0:T(8,128)(2,1)S(1)}, bf16[2,2,8,128]{3,2,1,0:T(8,128)(2,1)}, u32[]{:S(2)}) copy-start(bf16[2,2,8,128]{3,2,1,0:T(8,128)(2,1)} %new_keys.1) | copy-start | bytes 24580
  2.5 11.6 %copy-start.6 = (bf16[2,2,8,128]{3,2,1,0:T(8,128)(2,1)S(1)}, bf16[2,2,8,128]{3,2,1,0:T(8,128)(2,1)}, u32[]{:S(2)}) copy-start(bf16[2,2,8,128]{3,2,1,0:T(8,128)(2,1)} %new_values.1) | copy-start | bytes 24580
  2.6 32.0 %all-to-all-start = ((bf16[128,17,2,128]{3,2,1,0:T(2,128)(2,1)}), bf16[128,17,2,128]{3,2,1,0:T(2,128)(2,1)S(1)}, u32[]{:S(2)}, u32[]{:S(2)}) async-start(bf16[128,17,2,128]{3,2,1,0:T(2,128)(2,1)} %bitcast.11), calls=%async_computation | async-start | bytes 2228224 | tf_op jit(solution)/shard_map/all_to_all | solution.py:366
  18.6 0.6 copy-start.3
  19.3 0.5 copy-start.7
  40.5 23.8 %copy-start.4 = (f32[256,128]{1,0:T(8,128)S(1)}, f32[256,128]{1,0:T(8,128)}, u32[]{:S(2)}) copy-start(f32[256,128]{1,0:T(8,128)} %copy-done.3) | copy-start | bytes 393220
  40.5 23.8 %copy-start.8 = (s32[128]{0:T(128)S(1)}, s32[128]{0:T(128)}, u32[]{:S(2)}) copy-start(s32[128]{0:T(128)} %copy-done.7) | copy-start | bytes 1540

commit v4 on v3

--- a/solution.py
+++ b/solution.py
@@ -15,6 +15,7 @@
 SPAN = SLOTS * TILE + SLOTS
 PIECES = 3
 MIB = 1024 * 1024
+LOG2E = 1.4426950408889634
 
 
 def lane_iota(rows):
@@ -36,7 +37,7 @@
                 tiles[pl.ds(start, kv, stride=TILE), :] = block.astype(jnp.float32)
 
 
-def pack_kernel(owner_hbm, slot_hbm, queries_hbm, out, owner, slot, queries, tiles, wide, narrow, count, sems):
+def pack_kernel(owner_hbm, slot_hbm, queries_hbm, out, owner, slot, queries, tiles, wide, count, sems):
     devices = wide.shape[0] // SPAN
     seqs, kv, picks = owner.shape
     copies = [
@@ -67,17 +68,7 @@
                 wide[pl.ds(base + used[k] * TILE, TILE), :] = block
                 code = jnp.where(lane < LANES // 2, slot[s, g, k] + 1, g).astype(jnp.float32)
                 wide[pl.ds(base + SLOTS * TILE + used[k], 1), :] = code
-    parts = narrow.shape[0]
-    rows = narrow.shape[1]
-    copies = []
-    for i in range(parts):
-        narrow[i] = wide[i * rows : (i + 1) * rows, :].astype(narrow.dtype)
-        copies.append(
-            pltpu.make_async_copy(narrow.at[i], out.at[pl.ds(i * rows, rows)], sems.at[3 + i])
-        )
-        copies[-1].start()
-    for copy in copies:
-        copy.wait()
+    out[...] = wide[...].astype(out.dtype)
 
 
 def place_items(owner, place, count):
@@ -93,66 +84,56 @@
                 place[(s * kv + g) * picks + k] = to[k] * SLOTS + used[k]
 
 
-def local_kernel(
-    queries,
-    new_keys,
-    new_values,
-    keys,
-    values,
-    owner_hbm,
-    mixed,
-    level,
-    place,
-    tiles,
-    fresh,
-    owner,
-    count,
-    sem,
-):
-    copy = pltpu.make_async_copy(owner_hbm, owner, sem)
-    copy.start()
-    seqs, steps, kv, wide = queries.shape
-    group = wide // LANES
-    recent = keys.shape[2]
+def near_weights(queries, new_keys, keys, tiles):
+    seqs, steps, kv, width = queries.shape
+    group = width // LANES
     scale = LANES ** (-0.5)
     load_tiles(queries, tiles)
     news = seqs * steps * kv
-    for s in range(seqs):
-        for u in range(steps):
-            at = (s * steps + u) * kv
-            fresh[at : at + kv, :] = new_keys[s, u].astype(jnp.float32)
-            fresh[news + at : news + at + kv, :] = new_values[s, u].astype(jnp.float32)
-    fresh_keys = fresh[:news, :].astype(jnp.bfloat16)
-    fresh_values = jnp.concatenate(
-        [fresh[news:, :].astype(jnp.bfloat16), jnp.ones((news, LANES), jnp.bfloat16)], axis=1
-    )
-    ones = jnp.ones((recent, LANES), jnp.bfloat16)
+    fresh = [new_keys[s, u].astype(jnp.float32) for s in range(seqs) for u in range(steps)]
+    fresh = jnp.concatenate(fresh, axis=0).astype(jnp.bfloat16)
+    nt = (((1,), (1,)), ((), ()))
     col = lax.broadcasted_iota(jnp.int32, (TILE, news), 1)
     step = lax.broadcasted_iota(jnp.int32, (TILE, news), 0) // group
-    nt = (((1,), (1,)), ((), ()))
+    rows = tiles[...].astype(jnp.bfloat16)
+    late = lax.dot_general(rows, fresh, nt, preferred_element_type=jnp.float32)
+    spots = [(s, g, (s * kv + g) * TILE) for s in range(seqs) for g in range(kv)]
+    near = [
+        lax.dot_general(rows[at : at + TILE, :], keys[s, g], nt, preferred_element_type=jnp.float32)
+        for s, g, at in spots
+    ]
+    near_parts, late_parts, peaks = [], [], []
+    for (s, g, at), block in zip(spots, near):
+        first = s * steps * kv + g
+        seen = (col >= first) & (col <= first + step * kv) & (lax.rem(col, kv) == g)
+        tail = jnp.where(seen, late[at : at + TILE, :], FLOOR)
+        peak = jnp.maximum(
+            jnp.max(block, axis=1, keepdims=True), jnp.max(tail, axis=1, keepdims=True)
+        )
+        near_parts.append(jnp.exp2((block - peak) * (scale * LOG2E)).astype(jnp.bfloat16))
+        late_parts.append(jnp.exp2((tail - peak) * (scale * LOG2E)))
+        peaks.append(peak * scale)
+    return near_parts, jnp.concatenate(late_parts, axis=0).astype(jnp.bfloat16), peaks
+
+
+def near_sums(weights, new_values, values, mixed, level):
+    near_parts, late_parts, peaks = weights
+    seqs, steps, kv, _ = new_values.shape
+    fresh = [new_values[s, u].astype(jnp.float32) for s in range(seqs) for u in range(steps)]
+    fresh = jnp.concatenate(fresh, axis=0).astype(jnp.bfloat16)
+    fresh = jnp.concatenate([fresh, jnp.ones_like(fresh)], axis=1)
+    late = lax.dot(late_parts, fresh, preferred_element_type=jnp.float32)
+    ones = jnp.ones(values.shape[2:], jnp.bfloat16)
     for s in range(seqs):
         for g in range(kv):
-            at = (s * kv + g) * TILE
-            query = tiles[at : at + TILE, :].astype(jnp.bfloat16)
-            near = lax.dot_general(query, keys[s, g], nt, preferred_element_type=jnp.float32) * scale
-            late = lax.dot_general(query, fresh_keys, nt, preferred_element_type=jnp.float32) * scale
-            first = s * steps * kv + g
-            seen = (col >= first) & (col <= first + step * kv) & (lax.rem(col, kv) == g)
-            late = jnp.where(seen, late, FLOOR)
-            peak = jnp.maximum(
-                jnp.max(near, axis=1, keepdims=True), jnp.max(late, axis=1, keepdims=True)
-            )
-            near_weights = jnp.exp(near - peak).astype(jnp.bfloat16)
-            late_weights = jnp.exp(late - peak).astype(jnp.bfloat16)
+            tile = s * kv + g
+            at = tile * TILE
             both = jnp.concatenate([values[s, g], ones], axis=1)
-            total = lax.dot(near_weights, both, preferred_element_type=jnp.float32)
-            total = total + lax.dot(late_weights, fresh_values, preferred_element_type=jnp.float32)
-            weight = total[:, LANES:]
+            total = lax.dot(near_parts[tile], both, preferred_element_type=jnp.float32)
+            total = total + late[at : at + TILE, :]
             mixed[at : at + TILE, :] = total[:, :LANES]
-            level[at : at + TILE, :LANES] = jnp.broadcast_to(peak, (TILE, LANES))
-            level[at : at + TILE, LANES:] = weight
-    copy.wait()
-    place_items(owner, place, count)
+            level[at : at + TILE, :LANES] = jnp.broadcast_to(peaks[tile], (TILE, LANES))
+            level[at : at + TILE, LANES:] = total[:, LANES:]
 
 
 def read_codes(pages, got, codes):
@@ -192,11 +173,20 @@
     batch,
     ahead,
     fill_hbm,
+    owner_hbm,
     got,
     keys,
     values,
-    unused,
+    queries,
+    new_keys,
+    new_values,
+    recent_keys,
+    recent_values,
     out,
+    mixed,
+    level,
+    place_hbm,
+    tiles,
     wide,
     answer,
     sides,
@@ -205,6 +195,9 @@
     codes_v,
     codes,
     fill,
+    owner,
+    count,
+    place,
     sems,
     key_sems,
     value_sems,
@@ -214,10 +207,13 @@
     scale = LANES ** (-0.5)
     fill_copy = pltpu.make_async_copy(fill_hbm, fill, sems.at[0])
     fill_copy.start()
+    owner_copy = pltpu.make_async_copy(owner_hbm, owner, sems.at[2])
+    owner_copy.start()
     read_codes(fill.shape[0], got, codes_v)
     codes_copy = pltpu.make_async_copy(codes_v, codes, sems.at[1])
     codes_copy.start()
     wide[...] = got[...].astype(jnp.float32)
+    near = near_weights(queries, new_keys, recent_keys, tiles)
     fill_copy.wait()
     codes_copy.wait()
     nt = (((1,), (1,)), ((), ()))
@@ -232,7 +228,8 @@
     def pull(step):
         for a in range(batch):
             item = step * batch + a
-            where = codes[item % SLOTS, item // SLOTS] * kv + codes[SLOTS + item % SLOTS, item // SLOTS]
+            message, c = item // SLOTS, item % SLOTS
+            where = codes[c, message] * kv + codes[SLOTS + c, message]
             pltpu.make_async_copy(keys.at[where], near_keys.at[item], key_sems.at[step]).start()
             pltpu.make_async_copy(values.at[where], near_values.at[item], value_sems.at[step]).start()
 
@@ -240,18 +237,18 @@
         span = pl.ds(step * batch, batch)
         pltpu.make_async_copy(keys.at[pl.ds(0, batch)], near_keys.at[span], key_sems.at[step]).wait()
         pltpu.make_async_copy(values.at[pl.ds(0, batch)], near_values.at[span], value_sems.at[step]).wait()
-        spots, rows, fills, queries = [], [], [], []
+        spots, rows, fills, asking = [], [], [], []
         for a in range(batch):
             item = step * batch + a
             message, c = item // SLOTS, item % SLOTS
             spots.append(message * SPAN + c * TILE)
             rows.append(c * (batch // SLOTS) + a // SLOTS)
             fills.append(fill[codes[c, message]])
-            queries.append(wide[pl.ds(spots[a], TILE), :].astype(jnp.bfloat16))
+            asking.append(wide[pl.ds(spots[a], TILE), :].astype(jnp.bfloat16))
         scores = []
         for b in range(0, batch, per_score):
             block = lax.dot_general(
-                jnp.concatenate(queries[b : b + per_score], axis=0),
+                jnp.concatenate(asking[b : b + per_score], axis=0),
                 near_keys[pl.ds(step * batch + b, per_score)].reshape(per_score * page, LANES),
                 nt,
                 preferred_element_type=jnp.float32,
@@ -265,8 +262,8 @@
             live = (lane >= first) & (lane < first + fills[a])
             part = jnp.where(live, scores[a], FLOOR)
             peak = jnp.max(part, axis=1, keepdims=True)
-            peaks.append(peak * scale)
-            weights.append(jnp.exp((part - peak) * scale))
+            peaks.append(peak)
+            weights.append(jnp.exp2((part - peak) * (scale * LOG2E)))
         totals = []
         for b in range(0, batch, per_mix):
             mix = jnp.concatenate(weights[b : b + per_mix], axis=0).astype(jnp.bfloat16)
@@ -283,6 +280,7 @@
             for j in range(0, batch // SLOTS, 8):
                 first = c * (batch // SLOTS) + j
                 value = sides[first : first + 8, :]
+                value = jnp.where(front[:8], value * scale, value)
                 high = value.astype(jnp.bfloat16).astype(jnp.float32)
                 rest = value - high
                 middle = rest.astype(jnp.bfloat16).astype(jnp.float32)
@@ -294,13 +292,33 @@
 
     for step in range(ahead):
         pull(step)
+    owner_copy.wait()
+    near_sums(near, new_values, recent_values, mixed, level)
+    place_items(owner, place, count)
+    place_copy = pltpu.make_async_copy(place, place_hbm, sems.at[3])
+    place_copy.start()
     for step in range(rounds):
         if step + ahead < rounds:
             pull(step + ahead)
         attend(step)
-
-
-def merge_kernel(picks, batch, place_hbm, got, mixed, level, out, wide, merged, place, sem):
+    place_copy.wait()
+
+
+def merge_kernel(
+    picks,
+    batch,
+    place_hbm,
+    got,
+    mixed,
+    level,
+    out,
+    wide,
+    merged,
+    place,
+    ready,
+    sem,
+    back_sems,
+):
     seqs, steps, kv, width = out.shape
     group = width // LANES
     copy = pltpu.make_async_copy(place_hbm, place, sem)
@@ -338,14 +356,19 @@
             weight = functools.reduce(jnp.add, [w * x[:, LANES:] for w, x in zip(shares, rows)])
             merged[pl.ds(at, TILE), :] = total / weight
 
-    for step in range(seqs * kv // batch):
-        merge(step)
+    backs = []
     for s in range(seqs):
+        for step in range(s * kv // batch, (s + 1) * kv // batch):
+            merge(step)
         for t in range(steps):
             for h in range(group):
                 start = s * kv * TILE + t * group + h
                 block = merged[pl.ds(start, kv, stride=TILE), :]
-                out[s, t, :, h * LANES : (h + 1) * LANES] = block.astype(out.dtype)
+                ready[s, t, :, h * LANES : (h + 1) * LANES] = block.astype(ready.dtype)
+        backs.append(pltpu.make_async_copy(ready.at[s], out.at[s], back_sems.at[s]))
+        backs[-1].start()
+    for back in backs:
+        back.wait()
 
 
 VMEM = pl.BlockSpec(memory_space=pltpu.VMEM)
@@ -389,64 +412,40 @@
     tiles = pltpu.VMEM((tile_rows, LANES), jnp.float32)
     messages = jax.ShapeDtypeStruct((rows, LANES), jnp.bfloat16)
 
-    parts = 4
     asked = pl.pallas_call(
         pack_kernel,
-        out_shape=pltpu.HBM(messages.shape, messages.dtype),
+        out_shape=messages,
         in_specs=[ANY, ANY, ANY],
-        out_specs=ANY,
+        out_specs=VMEM,
         scratch_shapes=[
             pltpu.SMEM(top_owner.shape, jnp.int32),
             pltpu.SMEM(top_slot.shape, jnp.int32),
             pltpu.VMEM(queries.shape, queries.dtype),
             tiles,
             wide,
-            pltpu.VMEM((parts, rows // parts, LANES), messages.dtype),
             pltpu.SMEM((devices,), jnp.int32),
-            pltpu.SemaphoreType.DMA((3 + parts,)),
+            pltpu.SemaphoreType.DMA((3,)),
         ],
         compiler_params=params(16),
         name="pack",
     )(in_hbm(top_owner), in_hbm(top_slot), in_hbm(queries))
     asked = exchange(asked, devices)
 
-    mixed, level, place = pl.pallas_call(
-        local_kernel,
-        out_shape=(
-            jax.ShapeDtypeStruct((tile_rows, LANES), jnp.float32),
-            jax.ShapeDtypeStruct((tile_rows, 2 * LANES), jnp.float32),
-            jax.ShapeDtypeStruct((items,), jnp.int32),
-        ),
-        in_specs=[VMEM] * 5 + [ANY],
-        out_specs=(VMEM, VMEM, SMEM),
-        scratch_shapes=[
-            tiles,
-            pltpu.VMEM((2 * seqs * steps * kv, LANES), jnp.float32),
-            pltpu.SMEM(top_owner.shape, jnp.int32),
-            pltpu.SMEM((devices,), jnp.int32),
-            pltpu.SemaphoreType.DMA,
-        ],
-        compiler_params=params(16),
-        cost_estimate=pl.CostEstimate(flops=70_000_000, bytes_accessed=3_000_000, transcendentals=70_000),
-        name="near",
-    )(
-        queries,
-        new_keys,
-        new_values,
-        recent_keys,
-        recent_values,
-        in_hbm(top_owner),
-    )
-
     pool = (page_keys.shape[0] * kv, page_keys.shape[2], LANES)
     slots, batch = SLOTS * devices, 64
     pages = pltpu.VMEM((slots,) + pool[1:], page_keys.dtype)
-    answers = pl.pallas_call(
+    answers, mixed, level, place = pl.pallas_call(
         functools.partial(answer_kernel, kv, batch, 2),
-        out_shape=messages,
-        in_specs=[ANY, VMEM, ANY, ANY, ANY],
-        out_specs=VMEM,
+        out_shape=(
+            messages,
+            jax.ShapeDtypeStruct((tile_rows, LANES), jnp.float32),
+            jax.ShapeDtypeStruct((tile_rows, 2 * LANES), jnp.float32),
+            pltpu.HBM((items,), jnp.int32),
+        ),
+        in_specs=[ANY, ANY, VMEM, ANY, ANY] + [VMEM] * 5,
+        out_specs=(VMEM, VMEM, VMEM, ANY),
         scratch_shapes=[
+            tiles,
             wide,
             wide,
             pltpu.VMEM((batch, LANES), jnp.float32),
@@ -455,25 +454,41 @@
             pltpu.VMEM((8, LANES), jnp.int32),
             pltpu.SMEM((8, LANES), jnp.int32),
             pltpu.SMEM(page_fill.shape, jnp.int32),
-            pltpu.SemaphoreType.DMA((2,)),
+            pltpu.SMEM(top_owner.shape, jnp.int32),
+            pltpu.SMEM((devices,), jnp.int32),
+            pltpu.SMEM((items,), jnp.int32),
+            pltpu.SemaphoreType.DMA((4,)),
             pltpu.SemaphoreType.DMA((slots // batch,)),
             pltpu.SemaphoreType.DMA((slots // batch,)),
         ],
         compiler_params=params(24),
         name="answer",
-    )(in_hbm(page_fill), asked, in_hbm(page_keys.reshape(pool)), in_hbm(page_values.reshape(pool)), level)
+    )(
+        in_hbm(page_fill),
+        in_hbm(top_owner),
+        asked,
+        in_hbm(page_keys.reshape(pool)),
+        in_hbm(page_values.reshape(pool)),
+        queries,
+        new_keys,
+        new_values,
+        recent_keys,
+        recent_values,
+    )
     answers = exchange(answers, devices)
 
     return pl.pallas_call(
         functools.partial(merge_kernel, picks, 8),
         out_shape=jax.ShapeDtypeStruct(queries.shape, jnp.bfloat16),
         in_specs=[ANY, VMEM, VMEM, VMEM],
-        out_specs=VMEM,
+        out_specs=ANY,
         scratch_shapes=[
             wide,
             tiles,
             pltpu.SMEM((items,), jnp.int32),
+            pltpu.VMEM(queries.shape, jnp.bfloat16),
             pltpu.SemaphoreType.DMA,
+            pltpu.SemaphoreType.DMA((seqs,)),
         ],
         compiler_params=params(16),
         name="merge",

time: 66.9 us -> 66.2 us (0.990)
  blocking collectives: 23.8 us -> 55.3 us
  waiting for transfers between devices: 14.7 us -> 0 us
  starting transfers between devices: 11.5 us -> 0 us
  Pallas kernels: 15.3 us -> 10.5 us
  local copies, waits for them, and re-layouts: 1.19 us -> 0.04 us
    all_to_all x1 -> x2, blocking collectives: 23.8 us -> 55.3 us  [exchange(): boxed = lax.all_to_all(boxed, AXES, split_axis=0, concat_axis=0, tiled=True)]
    all_to_all x1 -> x0, waiting for transfers between devices: 14.7 us -> none  [exchange(): boxed = lax.all_to_all(boxed, AXES, split_axis=0, concat_axis=0, tiled=True)]
    all_to_all x1 -> x0, starting transfers between devices: 11.5 us -> none  [exchange(): boxed = lax.all_to_all(boxed, AXES, split_axis=0, concat_axis=0, tiled=True)]
    pallas_call x2 -> x1, Pallas kernels: 6.97 us -> 1.53 us  [on_device(): pl.pallas_call(pack_kernel, out_shape=messages, in_specs=[ANY, ANY, ANY],...]
    unnamed x18 -> x12, local copies, waits for them, and re-layouts: 1.19 us -> 0.04 us
    pallas_call x1, Pallas kernels: 6.01 us -> 6.73 us  [on_device(): pl.pallas_call(functools.partial(answer_kernel, kv, batch, 2), out_shape=...]
  transfers between devices with their start and end apart: 1 -> 0, of which waited for: 1 -> 0; matrix products, arithmetic and copies ran while one was open for 0% -> 0% of each run, Pallas kernels for 7% -> 0%
where the time goes in v4:
time: 66.2 us; the launch traced here: 66 us
  blocking collectives  55.3 us (84%)
  Pallas kernels  10.5 us (16%)
    all_to_all x2, blocking collectives, exchange(): boxed = lax.all_to_all(boxed, AXES, split_axis=0, concat_axis=0, tiled=True)  55.3 us
    pallas_call x1, Pallas kernels, on_device(): pl.pallas_call(functools.partial(answer_kernel, kv, batch, 2), out_shape=...  6.73 us
    pallas_call x1, Pallas kernels, on_device(): pl.pallas_call(functools.partial(merge_kernel, picks, 8), out_shape=jax.S...  2.28 us
    pallas_call x1, Pallas kernels, on_device(): pl.pallas_call(pack_kernel, out_shape=messages, in_specs=[ANY, ANY, ANY],...  1.53 us

profile of v4, /device:TPU:1, one launch (start us, length us, event | category | flops | bytes accessed | tf_op | source)
XLA Modules:
  0.0 66.0 jit_solution(3092784418819065666)
XLA Ops:
  0.0 1.5 %pack.1 = bf16[4352,128]{1,0:T(8,128)(2,1)S(1)} custom-call(s32[2,8,8]{2,1,0:T(8,128)} %owner_hbm.3, s32[2,8,8]{2,1,0:T(8,128)} %slot_hbm.1, bf16[2,2,8,1024]{3,2,1,0:T(8,128)(2,1)} %queries.1), custom_call_target="tpu_custom_call" | custom-call | tf_op jit(solution)/shard_map/pack/pallas_call | solution.py:415
  1.5 0.0 copy-start
  1.5 0.0 copy-start.1
  1.6 0.0 copy-start.2
  1.6 0.0 copy-start.3
  1.6 0.0 copy-start.4
  1.6 31.8 %all_to_all.10 = bf16[128,17,2,128]{3,2,1,0:T(2,128)(2,1)S(1)} all-to-all(bf16[128,17,2,128]{3,2,1,0:T(2,128)(2,1)S(1)} %bitcast.8), channel_id=1, replica_groups=mesh['ctx'=32,'rows'=4] {'ctx','rows'}, dimensions={0} | all-to-all | bytes 2228224 | tf_op jit(solution)/shard_map/all_to_all | solution.py:389
  33.4 0.0 copy-done
  33.4 0.0 copy-done.1
  33.4 0.0 copy-done.2
  33.4 0.0 copy-done.3
  33.4 0.0 copy-done.4
  33.4 6.7 %answer.1 = (bf16[4352,128]{1,0:T(8,128)(2,1)S(1)}, f32[256,128]{1,0:T(8,128)S(1)}, f32[256,256]{1,0:T(8,128)S(1)}, s32[128]{0:T(128)}) custom-call(s32[64]{0:T(128)} %fill_hbm.1, s32[2,8,8]{2,1,0:T(8,128)} %owner_hbm.3, bf16[4352,128]{1,0:T(8,128)(2,1)S(1)} %bitcast.6, bf16[512,64,128]{2,1,0:T(8,128)(2,1)} %bitcast.10, bf16[512,64,128]{2,1,0:T(8,128)(2,1)} %bitcast.11, ...), custom_call_target="tpu_custom_call" | custom-call | tf_op jit(solution)/shard_map/answer/pallas_call | solution.py:437
  40.1 0.0 copy-start.5
  40.1 23.5 %all_to_all.11 = bf16[128,17,2,128]{3,2,1,0:T(2,128)(2,1)S(1)} all-to-all(bf16[128,17,2,128]{3,2,1,0:T(2,128)(2,1)S(1)} %bitcast.9), channel_id=1, replica_groups=mesh['ctx'=32,'rows'=4] {'ctx','rows'}, dimensions={0} | all-to-all | bytes 2228224 | tf_op jit(solution)/shard_map/all_to_all | solution.py:389
  63.7 0.0 copy-done.5
  63.7 2.3 %merge.1 = bf16[2,2,8,1024]{3,2,1,0:T(8,128)(2,1)} custom-call(s32[128]{0:T(128)S(1)} %copy-done.5, bf16[4352,128]{1,0:T(8,128)(2,1)S(1)} %bitcast.7, f32[256,128]{1,0:T(8,128)S(1)} %get-tuple-element.11.mixed, f32[256,256]{1,0:T(8,128)S(1)} %get-tuple-element.12.level), custom_call_target="tpu_custom_call" | custom-call | tf_op jit(solution)/shard_map/merge/pallas_call | solution.py:480
Async XLA Ops:
  1.5 31.8 %copy-start = (bf16[2,8,256,128]{3,2,1,0:T(8,128)(2,1)S(1)}, bf16[2,8,256,128]{3,2,1,0:T(8,128)(2,1)}, u32[]{:S(2)}) copy-start(bf16[2,8,256,128]{3,2,1,0:T(8,128)(2,1)} %recent_keys.1) | copy-start | bytes 3145732
  1.5 31.8 %copy-start.1 = (bf16[2,8,256,128]{3,2,1,0:T(8,128)(2,1)S(1)}, bf16[2,8,256,128]{3,2,1,0:T(8,128)(2,1)}, u32[]{:S(2)}) copy-start(bf16[2,8,256,128]{3,2,1,0:T(8,128)(2,1)} %recent_values.1) | copy-start | bytes 3145732
  1.6 31.8 %copy-start.2 = (bf16[2,2,8,1024]{3,2,1,0:T(8,128)(2,1)S(1)}, bf16[2,2,8,1024]{3,2,1,0:T(8,128)(2,1)}, u32[]{:S(2)}) copy-start(bf16[2,2,8,1024]{3,2,1,0:T(8,128)(2,1)} %queries.1) | copy-start | bytes 196612
  1.6 31.8 %copy-start.3 = (bf16[2,2,8,128]{3,2,1,0:T(8,128)(2,1)S(1)}, bf16[2,2,8,128]{3,2,1,0:T(8,128)(2,1)}, u32[]{:S(2)}) copy-start(bf16[2,2,8,128]{3,2,1,0:T(8,128)(2,1)} %new_keys.1) | copy-start | bytes 24580
  1.6 31.8 %copy-start.4 = (bf16[2,2,8,128]{3,2,1,0:T(8,128)(2,1)S(1)}, bf16[2,2,8,128]{3,2,1,0:T(8,128)(2,1)}, u32[]{:S(2)}) copy-start(bf16[2,2,8,128]{3,2,1,0:T(8,128)(2,1)} %new_values.1) | copy-start | bytes 24580
  40.1 23.5 %copy-start.5 = (s32[128]{0:T(128)S(1)}, s32[128]{0:T(128)}, u32[]{:S(2)}) copy-start(s32[128]{0:T(128)} %get-tuple-element.9.place_hbm) | copy-start | bytes 1540

commit v5 on v4

--- a/solution.py
+++ b/solution.py
@@ -213,7 +213,6 @@
     codes_copy = pltpu.make_async_copy(codes_v, codes, sems.at[1])
     codes_copy.start()
     wide[...] = got[...].astype(jnp.float32)
-    near = near_weights(queries, new_keys, recent_keys, tiles)
     fill_copy.wait()
     codes_copy.wait()
     nt = (((1,), (1,)), ((), ()))
@@ -223,6 +222,7 @@
     per_score, per_mix = 4, 2
     ones = jnp.ones((per_mix * page, LANES), jnp.bfloat16)
     rounds = devices * SLOTS // batch
+    lane8 = lane_iota(8)
     piece = lax.rem(lane_iota(8) // TILE, PIECES)
 
     def pull(step):
@@ -259,8 +259,11 @@
         peaks, weights = [], []
         for a in range(batch):
             first = a * page % LANES
-            live = (lane >= first) & (lane < first + fills[a])
-            part = jnp.where(live, scores[a], FLOOR)
+            live = lane8 < first + fills[a]
+            if first:
+                live = live & (lane8 >= first)
+            part = [jnp.where(live, scores[a][i : i + 8, :], FLOOR) for i in range(0, TILE, 8)]
+            part = jnp.concatenate(part, axis=0)
             peak = jnp.max(part, axis=1, keepdims=True)
             peaks.append(peak)
             weights.append(jnp.exp2((part - peak) * (scale * LOG2E)))
@@ -292,6 +295,7 @@
 
     for step in range(ahead):
         pull(step)
+    near = near_weights(queries, new_keys, recent_keys, tiles)
     owner_copy.wait()
     near_sums(near, new_values, recent_values, mixed, level)
     place_items(owner, place, count)
@@ -478,7 +482,7 @@
     answers = exchange(answers, devices)
 
     return pl.pallas_call(
-        functools.partial(merge_kernel, picks, 8),
+        functools.partial(merge_kernel, picks, 4),
         out_shape=jax.ShapeDtypeStruct(queries.shape, jnp.bfloat16),
         in_specs=[ANY, VMEM, VMEM, VMEM],
         out_specs=ANY,

time: 66.2 us -> 66.1 us (level)
  no operation moved by 1% of the time
where the time goes in v5:
time: 66.1 us; the launch traced here: 65.9 us
  blocking collectives  55.2 us (84%)
  Pallas kernels  10.6 us (16%)
    all_to_all x2, blocking collectives, exchange(): boxed = lax.all_to_all(boxed, AXES, split_axis=0, concat_axis=0, tiled=True)  55.2 us
    pallas_call x1, Pallas kernels, on_device(): pl.pallas_call(functools.partial(answer_kernel, kv, batch, 2), out_shape=...  6.76 us
    pallas_call x1, Pallas kernels, on_device(): pl.pallas_call(functools.partial(merge_kernel, picks, 4), out_shape=jax.S...  2.28 us
    pallas_call x1, Pallas kernels, on_device(): pl.pallas_call(pack_kernel, out_shape=messages, in_specs=[ANY, ANY, ANY],...  1.53 us

profile of v5, /device:TPU:1, one launch (start us, length us, event | category | flops | bytes accessed | tf_op | source)
XLA Modules:
  0.0 65.9 jit_solution(9236792841769685092)
XLA Ops:
  0.0 1.5 %pack.1 = bf16[4352,128]{1,0:T(8,128)(2,1)S(1)} custom-call(s32[2,8,8]{2,1,0:T(8,128)} %owner_hbm.3, s32[2,8,8]{2,1,0:T(8,128)} %slot_hbm.1, bf16[2,2,8,1024]{3,2,1,0:T(8,128)(2,1)} %queries.1), custom_call_target="tpu_custom_call" | custom-call | tf_op jit(solution)/shard_map/pack/pallas_call | solution.py:419
  1.5 0.0 copy-start
  1.5 0.0 copy-start.1
  1.6 0.0 copy-start.2
  1.6 0.0 copy-start.3
  1.6 0.0 copy-start.4
  1.6 31.8 %all_to_all.10 = bf16[128,17,2,128]{3,2,1,0:T(2,128)(2,1)S(1)} all-to-all(bf16[128,17,2,128]{3,2,1,0:T(2,128)(2,1)S(1)} %bitcast.8), channel_id=1, replica_groups=mesh['ctx'=32,'rows'=4] {'ctx','rows'}, dimensions={0} | all-to-all | bytes 2228224 | tf_op jit(solution)/shard_map/all_to_all | solution.py:393
  33.4 0.0 copy-done
  33.4 0.0 copy-done.1
  33.4 0.0 copy-done.2
  33.4 0.0 copy-done.3
  33.4 0.0 copy-done.4
  33.4 6.8 %answer.1 = (bf16[4352,128]{1,0:T(8,128)(2,1)S(1)}, f32[256,128]{1,0:T(8,128)S(1)}, f32[256,256]{1,0:T(8,128)S(1)}, s32[128]{0:T(128)}) custom-call(s32[64]{0:T(128)} %fill_hbm.1, s32[2,8,8]{2,1,0:T(8,128)} %owner_hbm.3, bf16[4352,128]{1,0:T(8,128)(2,1)S(1)} %bitcast.6, bf16[512,64,128]{2,1,0:T(8,128)(2,1)} %bitcast.10, bf16[512,64,128]{2,1,0:T(8,128)(2,1)} %bitcast.11, ...), custom_call_target="tpu_custom_call" | custom-call | tf_op jit(solution)/shard_map/answer/pallas_call | solution.py:441
  40.2 0.0 copy-start.5
  40.2 23.4 %all_to_all.11 = bf16[128,17,2,128]{3,2,1,0:T(2,128)(2,1)S(1)} all-to-all(bf16[128,17,2,128]{3,2,1,0:T(2,128)(2,1)S(1)} %bitcast.9), channel_id=1, replica_groups=mesh['ctx'=32,'rows'=4] {'ctx','rows'}, dimensions={0} | all-to-all | bytes 2228224 | tf_op jit(solution)/shard_map/all_to_all | solution.py:393
  63.6 0.0 copy-done.5
  63.6 2.3 %merge.1 = bf16[2,2,8,1024]{3,2,1,0:T(8,128)(2,1)} custom-call(s32[128]{0:T(128)S(1)} %copy-done.5, bf16[4352,128]{1,0:T(8,128)(2,1)S(1)} %bitcast.7, f32[256,128]{1,0:T(8,128)S(1)} %get-tuple-element.11.mixed, f32[256,256]{1,0:T(8,128)S(1)} %get-tuple-element.12.level), custom_call_target="tpu_custom_call" | custom-call | tf_op jit(solution)/shard_map/merge/pallas_call | solution.py:484
Async XLA Ops:
  1.5 31.8 %copy-start = (bf16[2,8,256,128]{3,2,1,0:T(8,128)(2,1)S(1)}, bf16[2,8,256,128]{3,2,1,0:T(8,128)(2,1)}, u32[]{:S(2)}) copy-start(bf16[2,8,256,128]{3,2,1,0:T(8,128)(2,1)} %recent_keys.1) | copy-start | bytes 3145732
  1.5 31.8 %copy-start.1 = (bf16[2,8,256,128]{3,2,1,0:T(8,128)(2,1)S(1)}, bf16[2,8,256,128]{3,2,1,0:T(8,128)(2,1)}, u32[]{:S(2)}) copy-start(bf16[2,8,256,128]{3,2,1,0:T(8,128)(2,1)} %recent_values.1) | copy-start | bytes 3145732
  1.6 31.8 %copy-start.2 = (bf16[2,2,8,1024]{3,2,1,0:T(8,128)(2,1)S(1)}, bf16[2,2,8,1024]{3,2,1,0:T(8,128)(2,1)}, u32[]{:S(2)}) copy-start(bf16[2,2,8,1024]{3,2,1,0:T(8,128)(2,1)} %queries.1) | copy-start | bytes 196612
  1.6 31.8 %copy-start.3 = (bf16[2,2,8,128]{3,2,1,0:T(8,128)(2,1)S(1)}, bf16[2,2,8,128]{3,2,1,0:T(8,128)(2,1)}, u32[]{:S(2)}) copy-start(bf16[2,2,8,128]{3,2,1,0:T(8,128)(2,1)} %new_keys.1) | copy-start | bytes 24580
  1.6 31.8 %copy-start.4 = (bf16[2,2,8,128]{3,2,1,0:T(8,128)(2,1)S(1)}, bf16[2,2,8,128]{3,2,1,0:T(8,128)(2,1)}, u32[]{:S(2)}) copy-start(bf16[2,2,8,128]{3,2,1,0:T(8,128)(2,1)} %new_values.1) | copy-start | bytes 24580
  40.2 23.5 %copy-start.5 = (s32[128]{0:T(128)S(1)}, s32[128]{0:T(128)}, u32[]{:S(2)}) copy-start(s32[128]{0:T(128)} %get-tuple-element.9.place_hbm) | copy-start | bytes 1540
